TPU v7x, 32 devices: a whole 2x2x4 slice. The times are simulated.
32 devices in a mesh: section: 2 (over x), expert: 16 (over z, y, core).
Axes of the slice: x: 2, y: 2, z: 4, core: 2. Of those that a mesh axis runs over, the one named last changes fastest.
Arguments:
- grad_out: bfloat16 [2, 3072, 2048], P('section', 'expert'), may hold values from -6 to 6
- layer_input: bfloat16 [2, 3072, 2048], P('section', 'expert'), may hold values from -6 to 6
- routes: int32 [2, 3072, 8], P('section', 'expert'), may hold values from 0 to 63, as said below
- route_logits: float32 [2, 3072, 8], P('section', 'expert'), may hold values from -6 to 6
- gate_weight: bfloat16 [2, 16, 2048, 768], P('section', 'expert'), may hold values from -0.125 to 0.125
- up_weight: bfloat16 [2, 16, 2048, 768], P('section', 'expert'), may hold values from -0.125 to 0.125
- down_weight: bfloat16 [2, 16, 768, 2048], P('section', 'expert'), may hold values from -0.21875 to 0.21875
- router_weight: bfloat16 [2, 2048, 64], P('section'), may hold values from -0.125 to 0.125
Outputs:
- grad_in: bfloat16 [2, 3072, 2048], P('section', 'expert')
- route_logit_grad: float32 [2, 3072, 8], P('section', 'expert')
Inputs may be any that keep to these rules, and one draw needn't show every extreme that they name: `routes`: each token names 8 different experts. Among the tokens of one device no expert is named more than 48 times, and in every section one expert below 16 is named exactly 48 times by the tokens of every device of that section.
All inputs are finite; a program needn't handle non-finite values.
Results may differ from a plain program's by a relative error of at most 0.004.
Values may be sent and summed in bfloat16 or wider, within the bound.
A program may use at most 128 MiB of HBM per device.

v0:
```python
import jax
import jax.numpy as jnp
from jax import lax
from jax.sharding import PartitionSpec as P


def from_behind(shard, axis, by):
    size = lax.axis_size(axis)
    return lax.ppermute(shard, axis, [(i, (i + by) % size) for i in range(size)])


def expert_rows(inputs, grad_rows, w_gate, w_up, w_down):
    pre_gate = jnp.dot(inputs, w_gate, preferred_element_type=jnp.float32)
    pre_up = jnp.dot(inputs, w_up, preferred_element_type=jnp.float32)
    hidden_grad = jnp.dot(grad_rows, w_down.T, preferred_element_type=jnp.float32)
    sigmoid_gate = jax.nn.sigmoid(pre_gate)
    activation = pre_gate * sigmoid_gate
    weight_grad = jnp.sum(hidden_grad * activation * pre_up, axis=-1).astype(jnp.bfloat16)
    gate_grad = (
        hidden_grad * pre_up * sigmoid_gate * (1.0 + pre_gate * (1.0 - sigmoid_gate))
    ).astype(jnp.bfloat16)
    up_grad = (hidden_grad * activation).astype(jnp.bfloat16)
    pair_grad = jnp.dot(gate_grad, w_gate.T, preferred_element_type=jnp.float32) + jnp.dot(
        up_grad, w_up.T, preferred_element_type=jnp.float32
    )
    return (pair_grad.astype(jnp.bfloat16), weight_grad)


def per_device(
    grad_out, layer_input, routes, route_logits, gate_weight, up_weight, down_weight, router_weight
):
    token_count = layer_input.shape[1]
    width_model = layer_input.shape[2]
    top_count = routes.shape[2]
    expert_count = lax.axis_size("expert")
    every_expert = router_weight.shape[2]
    capacity = 2 * token_count * top_count // every_expert
    slots_all = expert_count * capacity
    w_gate = gate_weight[0, 0]
    w_up = up_weight[0, 0]
    w_down = down_weight[0, 0]
    w_router = router_weight[0]
    picks = routes[0]
    flat_routes = picks.reshape(-1)
    route_count = flat_routes.shape[0]
    onehot = (flat_routes[:, None] == jnp.arange(expert_count, dtype=jnp.int32)[None, :]).astype(
        jnp.int32
    )
    rank_inside = jnp.sum((jnp.cumsum(onehot, axis=0) - 1) * onehot, axis=1)
    slot_index = jnp.where(
        flat_routes < expert_count, flat_routes * capacity + rank_inside, slots_all
    )
    slot_owner = jnp.full((slots_all + 1,), route_count, jnp.int32)
    slot_owner = slot_owner.at[slot_index].set(jnp.arange(route_count, dtype=jnp.int32))[:slots_all]
    token_index = jnp.where(slot_owner < route_count, slot_owner // top_count, token_count)

    def pack_rows(source):
        padded = jnp.concatenate([source, jnp.zeros((1, width_model), source.dtype)], axis=0)
        return padded[token_index].reshape(expert_count, capacity, width_model)

    sent_inputs = pack_rows(layer_input[0])
    incoming = from_behind(grad_out, "section", -1)[0]
    inputs = lax.all_to_all(sent_inputs, "expert", split_axis=0, concat_axis=0, tiled=True)
    senders = inputs.shape[0]
    per_source = inputs.shape[1]
    pair_grad, weight_grad = expert_rows(
        inputs.reshape(-1, width_model),
        lax.all_to_all(
            pack_rows(incoming), "expert", split_axis=0, concat_axis=0, tiled=True
        ).reshape(-1, width_model),
        w_gate,
        w_up,
        w_down,
    )
    pair_rows = pair_grad.reshape(senders, per_source, width_model)
    pair_dots = weight_grad.reshape(senders, per_source)
    returned_rows, returned_dots = (
        lax.all_to_all(pair_rows, "expert", split_axis=0, concat_axis=0, tiled=True),
        lax.all_to_all(pair_dots, "expert", split_axis=0, concat_axis=0, tiled=True),
    )
    flat_rows = jnp.concatenate(
        [returned_rows.reshape(slots_all, width_model), jnp.zeros((1, width_model), jnp.bfloat16)],
        axis=0,
    )
    flat_dots = jnp.concatenate(
        [returned_dots.reshape(slots_all), jnp.zeros((1,), jnp.bfloat16)], axis=0
    )
    route_rows = flat_rows[slot_index].reshape(token_count, top_count, width_model)
    weight_grad = flat_dots[slot_index].reshape(token_count, top_count).astype(jnp.float32)
    exponent = jnp.exp(route_logits[0])
    route_weight = exponent / jnp.sum(exponent, axis=1, keepdims=True)
    expert_sum = jnp.sum(route_weight[:, :, None] * route_rows, axis=1)
    center = jnp.sum(route_weight * weight_grad, axis=1, keepdims=True)
    logit_grad = route_weight * (weight_grad - center)
    matches = picks[:, :, None] == jnp.arange(every_expert, dtype=jnp.int32)[None, None, :]
    dense_grad = jnp.sum(jnp.where(matches, logit_grad[:, :, None], 0.0), axis=1)
    router_grad = jnp.dot(
        dense_grad, w_router.astype(jnp.float32).T, precision=lax.Precision.HIGHEST
    )
    grad_in = (incoming.astype(jnp.float32) + expert_sum + router_grad).astype(jnp.bfloat16)
    return (grad_in[None], logit_grad[None])


def solution(mesh):
    in_specs = (
        P("section", "expert", None),
        P("section", "expert", None),
        P("section", "expert", None),
        P("section", "expert", None),
        P("section", "expert", None, None),
        P("section", "expert", None, None),
        P("section", "expert", None, None),
        P("section", None, None),
    )
    out_specs = (P("section", "expert", None), P("section", "expert", None))
    return jax.shard_map(
        per_device, mesh=mesh, in_specs=in_specs, out_specs=out_specs, check_vma=False
    )
```

profile of v0, /device:TPU:18, one launch (start us, length us, event | category | flops | bytes accessed | tf_op | source)
XLA Modules:
  0.0 314.2 jit_solution(10911795239483650648)
XLA Ops:
  0.6 0.0 copy-start
  0.6 0.9 broadcast_compare_fusion
  1.5 0.8 broadcast_multiply_fusion
  2.3 0.8 copy.31
  3.1 0.1 eq.44
  3.2 0.1 eq.40
  3.3 0.1 copy.29
  3.5 0.1 lt.40
  3.6 0.1 copy.30
  3.7 0.1 mul.65
  3.8 4.5 %reduce-window.6 = s32[16,12,128]{2,1,0:T(8,128)S(1)} reduce-window(s32[16,12,128]{2,1,0:T(8,128)S(1)} %fusion.17, s32[]{:T(128)} %constant.13.clone.1), window={size=1x1x128 pad=0_0x0_0x127_0}, to_apply=%region_1.2 | reduce-window | flops 3121152 | bytes 196612 | tf_op jit(solution)/shard_map/reduce-window
  8.4 0.4 slice_reduce_fusion
  8.8 0.2 reduce-window.9
  9.0 0.1 add_add_fusion
  9.2 6.2 %scatter_custom_fusion = s32[769]{0:T(1024)S(1)} fusion(s32[1536]{0:T(1024)S(1)} %fusion.20, s32[1536]{0:T(1024)S(1)} %iota.15, s32[]{:T(128)} %constant.12.clone.1), kind=kCustom, calls=%fused_computation.58 | custom fusion | bytes 3080 | tf_op jit(solution)/shard_map/scatter | solution.py:54
  15.4 2.1 concatenate.13
  17.5 8.4 %gather_fusion.1 = bf16[768,2048]{1,0:T(8,128)(2,1)} fusion(bf16[193,2048]{1,0:T(8,128)(2,1)} %concatenate.13, s32[1024]{0:T(1024)S(1)} %pad_clamp_fusion.1), kind=kCustom, calls=%fused_computation.1 | custom fusion | bytes 6294528 | tf_op jit(solution)/shard_map/gather | solution.py:59
  25.9 6.2 %all-to-all-start.1 = ((bf16[16,48,2048]{2,1,0:T(8,128)(2,1)}), bf16[16,48,2048]{2,1,0:T(8,128)(2,1)}, u32[]{:S(2)}, u32[]{:S(2)}) async-start(bf16[16,48,2048]{2,1,0:T(8,128)(2,1)} %bitcast.56), calls=%async_computation.1 | async-start | bytes 6291456 | tf_op jit(solution)/shard_map/all_to_all | solution.py:63
  32.1 0.5 collective-permute-start
  32.6 19.3 %collective-permute-done = bf16[1,192,2048]{2,1,0:T(8,128)(2,1)S(1)} collective-permute-done((bf16[1,192,2048]{2,1,0:T(8,128)(2,1)}, bf16[1,192,2048]{2,1,0:T(8,128)(2,1)S(1)}, u32[]{:S(2)}, u32[]{:S(2)}) %collective-permute-start) | collective-permute-done | bytes 786464 | tf_op jit(solution)/shard_map/ppermute | solution.py:9
  51.9 0.9 copy-done.1
  52.8 1.0 concatenate.12
  53.8 8.4 %gather_fusion = bf16[768,2048]{1,0:T(8,128)(2,1)} fusion(bf16[193,2048]{1,0:T(8,128)(2,1)} %concatenate.12, s32[1024]{0:T(1024)S(1)} %pad_clamp_fusion.1), kind=kCustom, calls=%fused_computation | custom fusion | bytes 6294528 | tf_op jit(solution)/shard_map/gather | solution.py:59
  62.2 40.1 %all-to-all-done.1 = bf16[16,48,2048]{2,1,0:T(8,128)(2,1)} async-done(((bf16[16,48,2048]{2,1,0:T(8,128)(2,1)}), bf16[16,48,2048]{2,1,0:T(8,128)(2,1)}, u32[]{:S(2)}, u32[]{:S(2)}) %all-to-all-start.1) | async-done | bytes 3145760 | tf_op jit(solution)/shard_map/all_to_all | solution.py:63
  102.3 4.7 %all-to-all-start = ((bf16[16,48,2048]{2,1,0:T(8,128)(2,1)}), bf16[16,48,2048]{2,1,0:T(8,128)(2,1)}, u32[]{:S(2)}, u32[]{:S(2)}) async-start(bf16[16,48,2048]{2,1,0:T(8,128)(2,1)} %bitcast.57), calls=%async_computation | async-start | bytes 6291456 | tf_op jit(solution)/shard_map/all_to_all | solution.py:68
  107.0 6.9 %fusion.3 = f32[768,768]{0,1:T(8,128)} fusion(bf16[768,2048]{1,0:T(8,128)(2,1)} %bitcast.8, bf16[1,1,2048,768]{3,2,1,0:T(8,128)(2,1)} %param.12), kind=kOutput, calls=%fused_computation.10 | convolution fusion | flops 2415919104 | bytes 8650752 | tf_op jit(solution)/shard_map/dot_general | solution.py:13
  113.9 63.3 %all-to-all-done = bf16[16,48,2048]{2,1,0:T(8,128)(2,1)} async-done(((bf16[16,48,2048]{2,1,0:T(8,128)(2,1)}), bf16[16,48,2048]{2,1,0:T(8,128)(2,1)}, u32[]{:S(2)}, u32[]{:S(2)}) %all-to-all-start) | async-done | bytes 3145760 | tf_op jit(solution)/shard_map/all_to_all | solution.py:68
  177.2 5.6 %fusion.8 = f32[768,768]{0,1:T(8,128)S(1)} fusion(bf16[768,2048]{1,0:T(8,128)(2,1)} %bitcast.4, bf16[1,1,768,2048]{3,2,1,0:T(8,128)(2,1)} %param.14), kind=kOutput, calls=%fused_computation.15 | convolution fusion | flops 2415919104 | bytes 8650752 | tf_op jit(solution)/shard_map/dot_general | solution.py:15
  182.9 0.0 copy-done
  182.9 0.0 copy-done.9
  182.9 0.0 copy-start.10
  182.9 0.0 copy-start.8
  182.9 6.0 %multiply_reduce_fusion = (bf16[768]{0:T(1024)(128)(2,1)S(1)}, f32[768,768]{0,1:T(8,128)S(1)}) fusion(f32[768,768]{0,1:T(8,128)S(1)} %fusion.8, f32[768,768]{0,1:T(8,128)S(1)} %copy-done.9, bf16[768,2048]{1,0:T(8,128)(2,1)} %bitcast.8, bf16[1,1,2048,768]{3,2,1,0:T(8,128)(2,1)S(1)} %copy-done), kind=kOutput, calls=%fused_computation.17 | convolution fusion | flops 2420047104 | bytes 13370880 | tf_op jit(solution)/shard_map/dot_general | solution.py:14
  188.9 0.0 copy-done.10
  188.9 0.0 copy-done.8
  188.9 5.8 %fusion.1 = f32[768,2048]{1,0:T(8,128)} fusion(bf16[1,1,2048,768]{3,2,1,0:T(8,128)(2,1)S(1)} %copy-done.8, f32[768,768]{0,1:T(8,128)S(1)} %copy-done.9, f32[768,768]{0,1:T(8,128)S(1)} %fusion.8, f32[768,768]{0,1:T(8,128)S(1)} %get-tuple-element.11), kind=kOutput, calls=%fused_computation.8 | convolution fusion | flops 2421817344 | bytes 16515072 | tf_op jit(solution)/shard_map/dot_general | solution.py:23
  194.8 0.7 convert_element_type.80
  195.5 4.7 %all-to-all-start.3 = ((bf16[16,1,48]{2,1,0:T(2,128)(2,1)}), bf16[16,1,48]{2,1,0:T(2,128)(2,1)S(1)}, u32[]{:S(2)}, u32[]{:S(2)}) async-start(bf16[16,1,48]{2,1,0:T(2,128)(2,1)} %convert_element_type.80), calls=%async_computation.3 | async-start | bytes 16384 | tf_op jit(solution)/shard_map/all_to_all | solution.py:79
  200.1 7.5 %add_convert_fusion = bf16[768,2048]{1,0:T(8,128)(2,1)} fusion(f32[768,2048]{1,0:T(8,128)} %fusion.1, bf16[1,1,2048,768]{3,2,1,0:T(8,128)(2,1)S(1)} %copy-done, f32[768,768]{0,1:T(8,128)} %copy-done.10, f32[768,768]{0,1:T(8,128)} %fusion.3), kind=kOutput, calls=%fused_computation.7 | convolution fusion | flops 2422603776 | bytes 17301504 | tf_op jit(solution)/shard_map/dot_general | solution.py:23
  207.6 0.0 all-to-all-done.3
  207.6 6.2 %all-to-all-start.2 = ((bf16[16,48,2048]{2,1,0:T(8,128)(2,1)}), bf16[16,48,2048]{2,1,0:T(8,128)(2,1)}, u32[]{:S(2)}, u32[]{:S(2)}) async-start(bf16[16,48,2048]{2,1,0:T(8,128)(2,1)} %bitcast.58), calls=%async_computation.2 | async-start | bytes 6291456 | tf_op jit(solution)/shard_map/all_to_all | solution.py:78
  213.8 0.0 copy-done.7
  213.8 0.0 copy-start.4
  213.8 0.1 copy.28
  213.9 0.0 copy-start.5
  213.9 0.1 exponential_reduce_fusion
  214.1 0.1 reshape.211
  214.2 9.5 %gather_fusion.3 = bf16[1536]{0:T(1024)(128)(2,1)S(1)} fusion(bf16[769]{0:T(1024)(128)(2,1)S(1)} %pad_maximum_fusion, s32[2048]{0:T(1024)S(1)} %pad_clamp_fusion), kind=kCustom, calls=%fused_computation.3 | custom fusion | bytes 12288 | tf_op jit(solution)/shard_map/gather | solution.py:89
  223.7 0.1 reshape.213
  223.8 0.0 copy-done.5
  223.8 0.1 reshape.214
  223.9 0.2 multiply_reduce_fusion.1
  224.1 0.7 subtract_multiply_fusion.1
  224.8 1.6 copy.34
  226.4 0.1 subtract_multiply_fusion
  226.5 0.7 copy.35
  227.2 0.0 copy-done.4
  227.2 0.8 select_reduce_fusion
  227.9 56.1 %all-to-all-done.2 = bf16[16,48,2048]{2,1,0:T(8,128)(2,1)} async-done(((bf16[16,48,2048]{2,1,0:T(8,128)(2,1)}), bf16[16,48,2048]{2,1,0:T(8,128)(2,1)}, u32[]{:S(2)}, u32[]{:S(2)}) %all-to-all-start.2) | async-done | bytes 3145760 | tf_op jit(solution)/shard_map/all_to_all | solution.py:78
  284.0 4.0 %concatenate.14 = bf16[769,2048]{1,0:T(8,128)(2,1)} pad(bf16[768,2048]{1,0:T(8,128)(2,1)} %bitcast.12, bf16[]{:T(256)} %constant.17.clone.1), padding=0_1x0_0 | pad | bytes 6295554 | tf_op jit(solution)/shard_map/concatenate | solution.py:81
  288.0 0.0 copy-done.6
  288.0 15.0 %gather_fusion.2 = bf16[1536,2048]{1,0:T(8,128)(2,1)} fusion(bf16[769,2048]{1,0:T(8,128)(2,1)} %concatenate.14, s32[2048]{0:T(1024)S(1)} %copy-done.6), kind=kCustom, calls=%fused_computation.2 | custom fusion | bytes 12589056 | tf_op jit(solution)/shard_map/gather | solution.py:88
  303.1 9.3 %fusion = f32[192,2048]{1,0:T(8,128)S(1)} fusion(bf16[1536,2048]{1,0:T(8,128)(2,1)} %gather_fusion.2, f32[192,8]{1,0:T(8,128)S(1)} %get-tuple-element.9), kind=kLoop, calls=%fused_computation.6 | loop fusion | flops 9043968 | bytes 7870464 | tf_op jit(solution)/shard_map/reduce_sum | solution.py:92
  312.4 1.8 fusion.12
  (17 shorter events, 0.2 us)
Async XLA Ops:
  0.6 182.2 %copy-start = (bf16[1,1,2048,768]{3,2,1,0:T(8,128)(2,1)S(1)}, bf16[1,1,2048,768]{3,2,1,0:T(8,128)(2,1)}, u32[]{:S(2)}) copy-start(bf16[1,1,2048,768]{3,2,1,0:T(8,128)(2,1)} %param.13) | copy-start | bytes 9437188
  25.9 76.4 %all-to-all-start.1 = ((bf16[16,48,2048]{2,1,0:T(8,128)(2,1)}), bf16[16,48,2048]{2,1,0:T(8,128)(2,1)}, u32[]{:S(2)}, u32[]{:S(2)}) async-start(bf16[16,48,2048]{2,1,0:T(8,128)(2,1)} %bitcast.56), calls=%async_computation.1 | async-start | bytes 6291456 | tf_op jit(solution)/shard_map/all_to_all | solution.py:63
  32.1 19.8 %collective-permute-start = (bf16[1,192,2048]{2,1,0:T(8,128)(2,1)}, bf16[1,192,2048]{2,1,0:T(8,128)(2,1)S(1)}, u32[]{:S(2)}, u32[]{:S(2)}) collective-permute-start(bf16[1,192,2048]{2,1,0:T(8,128)(2,1)} %param.8), channel_id=1, source_target_pairs={{0,16},{16,0},{1,17},{17,1},{2,18},{18,2},{3,19},{19,3},{4,20},{20... | collective-permute-start | bytes 2359304 | tf_op jit(solution)/shard_map/ppermute | solution.py:9
  51.9 0.9 copy-start.1
  102.3 74.9 %all-to-all-start = ((bf16[16,48,2048]{2,1,0:T(8,128)(2,1)}), bf16[16,48,2048]{2,1,0:T(8,128)(2,1)}, u32[]{:S(2)}, u32[]{:S(2)}) async-start(bf16[16,48,2048]{2,1,0:T(8,128)(2,1)} %bitcast.57), calls=%async_computation | async-start | bytes 6291456 | tf_op jit(solution)/shard_map/all_to_all | solution.py:68
  177.2 5.6 %copy-start.9 = (f32[768,768]{0,1:T(8,128)S(1)}, f32[768,768]{0,1:T(8,128)}, u32[]{:S(2)}) copy-start(f32[768,768]{0,1:T(8,128)} %fusion.3) | copy-start | bytes 7077892
  182.9 6.0 %copy-start.10 = (f32[768,768]{0,1:T(8,128)}, f32[768,768]{0,1:T(8,128)S(1)}, u32[]{:S(2)}) copy-start(f32[768,768]{0,1:T(8,128)S(1)} %fusion.8) | copy-start | bytes 7077892
  182.9 6.0 %copy-start.8 = (bf16[1,1,2048,768]{3,2,1,0:T(8,128)(2,1)S(1)}, bf16[1,1,2048,768]{3,2,1,0:T(8,128)(2,1)}, u32[]{:S(2)}) copy-start(bf16[1,1,2048,768]{3,2,1,0:T(8,128)(2,1)} %param.12) | copy-start | bytes 9437188
  195.5 12.2 %all-to-all-start.3 = ((bf16[16,1,48]{2,1,0:T(2,128)(2,1)}), bf16[16,1,48]{2,1,0:T(2,128)(2,1)S(1)}, u32[]{:S(2)}, u32[]{:S(2)}) async-start(bf16[16,1,48]{2,1,0:T(2,128)(2,1)} %convert_element_type.80), calls=%async_computation.3 | async-start | bytes 16384 | tf_op jit(solution)/shard_map/all_to_all | solution.py:79
  207.6 6.2 %copy-start.7 = (f32[1,192,8]{1,2,0:T(8,128)S(1)}, f32[1,192,8]{1,2,0:T(8,128)}, u32[]{:S(2)}) copy-start(f32[1,192,8]{1,2,0:T(8,128)} %param.11) | copy-start | bytes 18436
  207.6 76.4 %all-to-all-start.2 = ((bf16[16,48,2048]{2,1,0:T(8,128)(2,1)}), bf16[16,48,2048]{2,1,0:T(8,128)(2,1)}, u32[]{:S(2)}, u32[]{:S(2)}) async-start(bf16[16,48,2048]{2,1,0:T(8,128)(2,1)} %bitcast.58), calls=%async_computation.2 | async-start | bytes 6291456 | tf_op jit(solution)/shard_map/all_to_all | solution.py:78
  213.8 13.4 %copy-start.4 = (s32[1,192,8]{1,2,0:T(8,128)S(1)}, s32[1,192,8]{1,2,0:T(8,128)}, u32[]{:S(2)}) copy-start(s32[1,192,8]{1,2,0:T(8,128)} %param.10) | copy-start | bytes 18436
  213.9 9.8 %copy-start.5 = (s32[2048]{0:T(1024)}, s32[2048]{0:T(1024)S(1)}, u32[]{:S(2)}) copy-start(s32[2048]{0:T(1024)S(1)} %pad_clamp_fusion) | copy-start | bytes 24580
  284.0 4.0 %copy-start.6 = (s32[2048]{0:T(1024)S(1)}, s32[2048]{0:T(1024)}, u32[]{:S(2)}) copy-start(s32[2048]{0:T(1024)} %copy-done.5) | copy-start | bytes 24580
  303.1 9.3 %copy-start.2 = (bf16[1,192,2048]{2,1,0:T(8,128)(2,1)S(1)}, bf16[1,192,2048]{2,1,0:T(8,128)(2,1)}, u32[]{:S(2)}) copy-start(bf16[1,192,2048]{2,1,0:T(8,128)(2,1)} %copy-done.1) | copy-start | bytes 2359300
  303.1 9.3 %copy-start.3 = (bf16[1,2048,64]{1,2,0:T(8,128)(2,1)S(1)}, bf16[1,2048,64]{1,2,0:T(8,128)(2,1)}, u32[]{:S(2)}) copy-start(bf16[1,2048,64]{1,2,0:T(8,128)(2,1)} %param.15) | copy-start | bytes 786436
where the time goes:
time: 315 us; the launch traced here: 314 us
  waiting for transfers between devices  179 us (57%)
  local copies, waits for them, and re-layouts  60.7 us (19%)
  matrix products  33.7 us (11%)
  starting transfers between devices  22.2 us (7%)
  other arithmetic  17.9 us (6%)
    all_to_all x1, waiting for transfers between devices, per_device(): lax.all_to_all(pack_rows(incoming), 'expert', split_axis=0, concat_axis=0...  63.3 us
    all_to_all x1, waiting for transfers between devices, per_device(): lax.all_to_all(pair_rows, 'expert', split_axis=0, concat_axis=0, tiled=True)  56.1 us
    all_to_all x1, waiting for transfers between devices, per_device(): lax.all_to_all(sent_inputs, 'expert', split_axis=0, concat_axis=0, tiled=...  40.1 us
    ppermute x1, waiting for transfers between devices, from_behind(): lax.ppermute(shard, axis, [(i, (i + by) % size) for i in range(size)])  19.3 us
    gather x2, local copies, waits for them, and re-layouts, pack_rows(): return padded[token_index].reshape(expert_count, capacity, width_model)  16.8 us
    gather x1, local copies, waits for them, and re-layouts, per_device(): flat_rows[slot_index].reshape(token_count, top_count, width_model)  15 us
    gather x1, local copies, waits for them, and re-layouts, per_device(): flat_dots[slot_index].reshape(token_count, top_count).astype(jnp.float32)  9.46 us
    reduce_sum x1, other arithmetic, per_device(): expert_sum = jnp.sum(route_weight[:, :, None] * route_rows, axis=1)  9.3 us
  transfers between devices with their start and end apart: 5, of which 4 were waited for; matrix products, arithmetic and copies ran while one was open for 12% of the time, Pallas kernels for 0%

commit v1 on v0

v1 whole, which is shorter than its diff:
```python
import functools

import jax
import jax.numpy as jnp
from jax import lax
from jax.experimental import pallas as pl
from jax.experimental.pallas import tpu as pltpu
from jax.sharding import PartitionSpec as P

MESH = pl.DeviceIdType.MESH
LINE = 4
LANES = 128
F32 = jnp.float32
BF16 = jnp.bfloat16


def dot_nt(a, b):
    return lax.dot_general(a, b, (((1,), (1,)), ((), ())), preferred_element_type=F32)


def dot_tn(a, b):
    return lax.dot_general(a, b, (((0,), (0,)), ((), ())), preferred_element_type=F32)


def kernel(
    sections, experts, cap,
    x_ref, grad_ref, routes_ref, logits_ref, gate_ref, up_ref, down_ref,
    total_ref, dots_ref,
    both, pack, rows, ret, back, part, fold, fold_in, meta, w_gate, w_up, w_down,
    x_local, w_sem, own_send, line_send, line_recv, meta_send, meta_recv,
    pack_send, pack_recv, ret_send, ret_recv, fold_send, fold_recv, perm_sem,
):
    group = experts // LINE
    tokens, width = both.shape[2], both.shape[3]
    top = routes_ref.shape[0]
    section = lax.axis_index("section")
    me = lax.axis_index("expert")
    p = me // group
    q = me % group
    far = LINE - 1 - p
    before = (section + sections - 1) % sections
    after = (section + 1) % sections

    def at(line, slot):
        return (section, line * group + slot)

    barrier = pltpu.get_barrier_semaphore()
    for step in range(1, LINE):
        pl.semaphore_signal(barrier, inc=1, device_id=at((p + step) % LINE, q), device_id_type=MESH)
    for step in range(1, group):
        pl.semaphore_signal(barrier, inc=1, device_id=at(p, (q + step) % group), device_id_type=MESH)
    for other in (before, after):
        pl.semaphore_signal(barrier, inc=1, device_id=(other, me), device_id_type=MESH)
    weights = [
        pltpu.make_async_copy(src, dst, w_sem.at[n])
        for n, (src, dst) in enumerate(((gate_ref, w_gate), (up_ref, w_up), (down_ref, w_down)))
    ]
    keep_x = pltpu.make_async_copy(x_ref, both.at[0, p], x_local)
    keep_x.start()
    pl.semaphore_wait(barrier, LINE + group)

    def own_x(way):
        return pltpu.make_async_remote_copy(
            src_ref=x_ref, dst_ref=both.at[0, p], send_sem=own_send.at[way],
            recv_sem=line_recv.at[0, p], device_id=at((p + (1, LINE - 1)[way]) % LINE, q),
            device_id_type=MESH,
        )

    def line_copy(kind, origin, way):
        return pltpu.make_async_remote_copy(
            src_ref=both.at[kind, origin], dst_ref=both.at[kind, origin],
            send_sem=line_send.at[kind, origin, way], recv_sem=line_recv.at[kind, origin],
            device_id=at((p + (1, LINE - 1)[way]) % LINE, q), device_id_type=MESH,
        )

    def has(way):
        return (p < LINE - 1) if way == 0 else (p > 0)

    for way in range(2):
        @pl.when(has(way))
        def _():
            own_x(way).start()
    permute = pltpu.make_async_remote_copy(
        src_ref=grad_ref, dst_ref=both.at[1, p], send_sem=perm_sem.at[0], recv_sem=perm_sem.at[1],
        device_id=(before, me), device_id_type=MESH,
    )
    permute.start()

    routes = routes_ref[...]
    exponent = jnp.exp(logits_ref[...])
    share = exponent / jnp.sum(exponent, axis=0, keepdims=True)
    expert_at = lax.broadcasted_iota(jnp.int32, (experts, tokens), 0)
    named = jnp.zeros((experts, tokens), F32)
    weight = jnp.zeros((experts, tokens), F32)
    for k in range(top):
        hit = routes[k:k + 1, :] == expert_at
        named = named + jnp.where(hit, 1.0, 0.0)
        weight = weight + jnp.where(hit, share[k:k + 1, :], 0.0)
    earlier = (
        lax.broadcasted_iota(jnp.int32, (tokens, tokens), 0)
        < lax.broadcasted_iota(jnp.int32, (tokens, tokens), 1)
    )
    rank = jnp.dot(
        named.astype(BF16), jnp.where(earlier, 1.0, 0.0).astype(BF16), preferred_element_type=F32
    )
    meta[p, 0] = jnp.where(named > 0.5, rank, -1.0)
    meta[p, 1] = weight

    def meta_copy(step):
        return pltpu.make_async_remote_copy(
            src_ref=meta.at[p], dst_ref=meta.at[p], send_sem=meta_send.at[step],
            recv_sem=meta_recv.at[step], device_id=at((p + step) % LINE, q), device_id_type=MESH,
        )

    def meta_wait(step):
        slot = (p + LINE - step) % LINE
        return pltpu.make_async_remote_copy(
            src_ref=meta.at[slot], dst_ref=meta.at[slot], send_sem=meta_send.at[step],
            recv_sem=meta_recv.at[step], device_id=at((p + step) % LINE, q), device_id_type=MESH,
        )

    for step in range(1, LINE):
        meta_copy(step).start()
    for copy in weights:
        copy.start()

    def chosen(origin, what, slot):
        table = meta[origin, what]
        return jnp.sum(jnp.where(expert_at == p * group + slot, table, 0.0), axis=0, keepdims=True)

    place = lax.broadcasted_iota(jnp.int32, (cap, tokens), 0).astype(F32)

    def pack_copy(kind, origin, step):
        return pltpu.make_async_remote_copy(
            src_ref=pack.at[kind, origin, step - 1],
            dst_ref=rows.at[kind, origin, q],
            send_sem=pack_send.at[kind, origin, step],
            recv_sem=pack_recv.at[kind, origin, step],
            device_id=at(p, (q + step) % group), device_id_type=MESH,
        )

    def pack_wait(kind, origin, step):
        return pltpu.make_async_remote_copy(
            src_ref=pack.at[kind, origin, step - 1],
            dst_ref=rows.at[kind, origin, (q + group - step) % group],
            send_sem=pack_send.at[kind, origin, step],
            recv_sem=pack_recv.at[kind, origin, step],
            device_id=at(p, (q + step) % group), device_id_type=MESH,
        )

    def do_pack(kind, origin):
        source = both[kind, origin]
        for step in list(range(1, group)) + [0]:
            pick = jnp.where(chosen(origin, 0, (q + step) % group) == place, 1.0, 0.0).astype(BF16)
            packed = jnp.dot(pick, source, preferred_element_type=F32).astype(BF16)
            if step == 0:
                rows[kind, origin, q] = packed
            else:
                pack[kind, origin, step - 1] = packed
                pack_copy(kind, origin, step).start()

    def ret_copy(origin, step):
        slot = (q + group - step) % group
        return pltpu.make_async_remote_copy(
            src_ref=ret.at[origin, slot], dst_ref=back.at[origin, q],
            send_sem=ret_send.at[origin, step], recv_sem=ret_recv.at[origin, step],
            device_id=at(p, slot), device_id_type=MESH,
        )

    def ret_wait(origin, step):
        return pltpu.make_async_remote_copy(
            src_ref=ret.at[origin, (q + group - step) % group],
            dst_ref=back.at[origin, (q + step) % group],
            send_sem=ret_send.at[origin, step], recv_sem=ret_recv.at[origin, step],
            device_id=at(p, (q + group - step) % group), device_id_type=MESH,
        )

    def do_expert(origin):
        for kind in range(2):
            for step in range(1, group):
                pack_wait(kind, origin, step).wait_recv()
        inputs = rows[0, origin].reshape(group * cap, width)
        grads = rows[1, origin].reshape(group * cap, width)
        pre_gate = jnp.dot(inputs, w_gate[...], preferred_element_type=F32)
        pre_up = jnp.dot(inputs, w_up[...], preferred_element_type=F32)
        hidden = dot_nt(grads, w_down[...])
        sigmoid = jax.nn.sigmoid(pre_gate)
        active = pre_gate * sigmoid
        up_grad = hidden * active
        dots = jnp.sum(up_grad * pre_up, axis=1, keepdims=True)
        gate_grad = hidden * pre_up * sigmoid * (1.0 + pre_gate * (1.0 - sigmoid))
        pair = dot_nt(gate_grad.astype(BF16), w_gate[...]) + dot_nt(up_grad.astype(BF16), w_up[...])
        lane = lax.broadcasted_iota(jnp.int32, (group * cap, LANES), 1)
        ret[origin, :, :, :width] = pair.astype(BF16).reshape(group, cap, width)
        ret[origin, :, :, width:] = (
            jnp.where(lane == me, dots, 0.0).astype(BF16).reshape(group, cap, LANES)
        )
        for step in range(1, group):
            ret_copy(origin, step).start()
        back[origin, q] = ret[origin, q]

    def fold_copy(origin, way):
        target = p + 1 - 2 * way
        if way == 0:
            slot = jnp.where(origin == target, LINE, origin)
        else:
            slot = origin
        return pltpu.make_async_remote_copy(
            src_ref=fold.at[origin], dst_ref=fold_in.at[slot],
            send_sem=fold_send.at[origin], recv_sem=fold_recv.at[slot],
            device_id=at((p + (1, LINE - 1)[way]) % LINE, q), device_id_type=MESH,
        )

    def fold_wait(slot):
        return pltpu.make_async_remote_copy(
            src_ref=fold.at[0], dst_ref=fold_in.at[slot],
            send_sem=fold_send.at[0], recv_sem=fold_recv.at[slot],
            device_id=at((p + 1) % LINE, q), device_id_type=MESH,
        )

    def do_combine(origin):
        for step in range(1, group):
            ret_wait(origin, step).wait_recv()
        picks, highs, lows = [], [], []
        for slot in range(group):
            hit = chosen(origin, 0, slot) == place
            weigh = jnp.where(hit, chosen(origin, 1, slot), 0.0)
            high = weigh.astype(BF16)
            picks.append(jnp.where(hit, 1.0, 0.0).astype(BF16))
            highs.append(high)
            lows.append((weigh - high.astype(F32)).astype(BF16))
        pick, high, low = (jnp.concatenate(parts, axis=0) for parts in (picks, highs, lows))
        came = back[origin, :, :, :width].reshape(group * cap, width)
        marks = back[origin, :, :, width:].reshape(group * cap, LANES)
        part[origin, :, :width] = dot_tn(high, came) + dot_tn(low, came)
        part[origin, :, width:] = dot_tn(pick, marks)

        @pl.when((p == LINE - 1) & (origin < p))
        def _():
            fold[origin] = part[origin].astype(BF16)
            fold_copy(origin, 1).start()

        @pl.when((p == 0) & (origin > p))
        def _():
            fold[origin] = part[origin].astype(BF16)
            fold_copy(origin, 0).start()

    keep_x.wait()
    do_pack(0, p)
    for step in range(1, LINE):
        meta_wait(step).wait_recv()
    permute.wait_recv()

    def arrival(way, i):
        count = p if way == 0 else far
        kind = jnp.where(i >= count, 1, 0)
        if way == 0:
            origin = jnp.where(i >= count, i - count, p - 1 - i)
        else:
            origin = jnp.where(i >= count, LINE - 1 - (i - count), p + 1 + i)
        valid = (i >= 0) & (i < 2 * count)
        return valid, kind, jnp.clip(origin, 0, LINE - 1)

    def candidate(n, i):
        valid_up, kind_up, origin_up = arrival(0, i)
        valid_down, kind_down, origin_down = arrival(1, i)
        valid = jnp.where(n == 0, jnp.where(i == 0, 1, 0), jnp.where(
            n == 1, jnp.where(valid_up, 1, 0), jnp.where(valid_down, 1, 0)))
        kind = jnp.where(n == 0, 1, jnp.where(n == 1, kind_up, kind_down))
        origin = jnp.where(n == 0, p, jnp.where(n == 1, origin_up, origin_down))
        return valid == 1, kind, origin

    def turn(i, carry):
        for way in range(2):
            valid, kind, origin = arrival(way, i)

            @pl.when(valid)
            def _():
                line_copy(kind, origin, way).wait_recv()

                @pl.when(has(way))
                def _():
                    line_copy(kind, origin, way).start()

            count = p if way == 0 else far

            @pl.when((i == 2 * count) & has(way))
            def _():
                line_copy(1, p, way).start()

        def each(step, body):
            def one(n, carry):
                valid, kind, origin = candidate(n, step)
                body(valid, kind, origin)
                return carry

            lax.fori_loop(0, 3, one, 0)

        def pack_one(valid, kind, origin):
            @pl.when(valid)
            def _():
                do_pack(kind, origin)

        def combine_one(valid, kind, origin):
            @pl.when(valid & (kind == 1))
            def _():
                do_combine(origin)

        def expert_one(valid, kind, origin):
            @pl.when(valid & (kind == 1))
            def _():
                do_expert(origin)

        each(i, pack_one)
        each(i - 1, combine_one)

        @pl.when(i == 0)
        def _():
            for copy in weights:
                copy.wait()

        each(i, expert_one)
        return carry

    lax.fori_loop(0, 2 * LINE - 1, turn, 0)

    def gather_back(r, carry):
        @pl.when((p < LINE - 1) & (r <= p))
        def _():
            fold_wait(r).wait_recv()
            part[r] = part[r] + fold_in[r].astype(F32)

            @pl.when(r < p)
            def _():
                fold[r] = part[r].astype(BF16)
                fold_copy(r, 1).start()

        origin = LINE - 1 - r

        @pl.when((p > 0) & (origin >= p))
        def _():
            slot = jnp.where(origin == p, LINE, origin)
            fold_wait(slot).wait_recv()
            part[origin] = part[origin] + fold_in[slot].astype(F32)

            @pl.when(origin > p)
            def _():
                fold[origin] = part[origin].astype(BF16)
                fold_copy(origin, 0).start()

        return carry

    lax.fori_loop(0, LINE, gather_back, 0)
    total_ref[...] = part[p, :, :width] + both[1, p].astype(F32)
    dots_ref[...] = part[p, :, width:]

    permute.wait_send()
    for step in range(1, LINE):
        meta_copy(step).wait_send()
    for way in range(2):
        @pl.when(has(way))
        def _():
            own_x(way).wait_send()
            line_copy(1, p, way).wait_send()

    def finish(origin, carry):
        for kind in range(2):
            for step in range(1, group):
                pack_copy(kind, origin, step).wait_send()

            @pl.when((origin < p) & has(0))
            def _():
                line_copy(kind, origin, 0).wait_send()

            @pl.when((origin > p) & has(1))
            def _():
                line_copy(kind, origin, 1).wait_send()

        for step in range(1, group):
            ret_copy(origin, step).wait_send()

        @pl.when(origin < p)
        def _():
            fold_copy(origin, 1).wait_send()

        @pl.when(origin > p)
        def _():
            fold_copy(origin, 0).wait_send()

        return carry

    lax.fori_loop(0, LINE, finish, 0)


def exchange(sections, x, grad, routes, logits, w_gate, w_up, w_down, capacity):
    tokens, width = x.shape
    hidden = w_gate.shape[1]
    experts = lax.axis_size("expert")
    group = experts // LINE
    cap = -(-capacity // 16) * 16
    wide = width + LANES
    vmem = pl.BlockSpec(memory_space=pltpu.VMEM)
    anywhere = pl.BlockSpec(memory_space=pl.ANY)
    dma = pltpu.SemaphoreType.DMA
    flops = 2 * LINE * group * cap * width * hidden * 5
    return pl.pallas_call(
        functools.partial(kernel, sections, experts, cap),
        out_shape=(
            jax.ShapeDtypeStruct((tokens, width), F32),
            jax.ShapeDtypeStruct((tokens, LANES), F32),
        ),
        in_specs=[anywhere, anywhere, vmem, vmem, anywhere, anywhere, anywhere],
        out_specs=(vmem, vmem),
        scratch_shapes=[
            pltpu.VMEM((2, LINE, tokens, width), BF16),
            pltpu.VMEM((2, LINE, group - 1, cap, width), BF16),
            pltpu.VMEM((2, LINE, group, cap, width), BF16),
            pltpu.VMEM((LINE, group, cap, wide), BF16),
            pltpu.VMEM((LINE, group, cap, wide), BF16),
            pltpu.VMEM((LINE, tokens, wide), F32),
            pltpu.VMEM((LINE, tokens, wide), BF16),
            pltpu.VMEM((LINE + 1, tokens, wide), BF16),
            pltpu.VMEM((LINE, 2, experts, tokens), F32),
            pltpu.VMEM((width, hidden), BF16),
            pltpu.VMEM((width, hidden), BF16),
            pltpu.VMEM((hidden, width), BF16),
            dma(()),
            dma((3,)),
            dma((2,)),
            dma((2, LINE, 2)),
            dma((2, LINE)),
            dma((LINE,)),
            dma((LINE,)),
            dma((2, LINE, group)),
            dma((2, LINE, group)),
            dma((LINE, group)),
            dma((LINE, group)),
            dma((LINE,)),
            dma((LINE + 1,)),
            dma((2,)),
        ],
        compiler_params=pltpu.CompilerParams(
            collective_id=0, has_side_effects=True, vmem_limit_bytes=63 * 1024 * 1024
        ),
        cost_estimate=pl.CostEstimate(
            flops=flops, bytes_accessed=2 * 3 * width * hidden, transcendentals=0
        ),
    )(x, grad, routes, logits, w_gate, w_up, w_down)


def per_device(
    grad_out, layer_input, routes, route_logits, gate_weight, up_weight, down_weight, router_weight
):
    token_count = layer_input.shape[1]
    top_count = routes.shape[2]
    every_expert = router_weight.shape[2]
    capacity = 2 * token_count * top_count // every_expert
    w_router = router_weight[0]
    picks = routes[0]
    total, dots = exchange(
        lax.axis_size("section"), layer_input[0], grad_out[0], picks.T, route_logits[0].T,
        gate_weight[0, 0], up_weight[0, 0], down_weight[0, 0], capacity,
    )
    exponent = jnp.exp(route_logits[0])
    route_weight = exponent / jnp.sum(exponent, axis=1, keepdims=True)
    lane = jnp.arange(LANES, dtype=jnp.int32)[None, None, :]
    weight_grad = jnp.sum(jnp.where(picks[:, :, None] == lane, dots[:, None, :], 0.0), axis=2)
    center = jnp.sum(route_weight * weight_grad, axis=1, keepdims=True)
    logit_grad = route_weight * (weight_grad - center)
    matches = picks[:, :, None] == jnp.arange(every_expert, dtype=jnp.int32)[None, None, :]
    dense_grad = jnp.sum(jnp.where(matches, logit_grad[:, :, None], 0.0), axis=1)
    router_grad = jnp.dot(
        dense_grad, w_router.astype(jnp.float32).T, precision=lax.Precision.HIGHEST
    )
    grad_in = (total + router_grad).astype(jnp.bfloat16)
    return (grad_in[None], logit_grad[None])


def solution(mesh):
    in_specs = (
        P("section", "expert", None),
        P("section", "expert", None),
        P("section", "expert", None),
        P("section", "expert", None),
        P("section", "expert", None, None),
        P("section", "expert", None, None),
        P("section", "expert", None, None),
        P("section", None, None),
    )
    out_specs = (P("section", "expert", None), P("section", "expert", None))
    return jax.shard_map(
        per_device, mesh=mesh, in_specs=in_specs, out_specs=out_specs, check_vma=False
    )
```

time: 315 us -> 231 us (0.73)
  Pallas kernels: 0 us -> 223 us
  waiting for transfers between devices: 179 us -> 0 us
  local copies, waits for them, and re-layouts: 60.7 us -> 0.88 us
  matrix products: 33.7 us -> 3.12 us
  starting transfers between devices: 22.2 us -> 0 us
  other arithmetic: 17.9 us -> 2.87 us
    pallas_call x0 -> x1, Pallas kernels: none -> 223 us  [exchange(): pl.pallas_call(functools.partial(kernel, sections, experts, cap), out_sha...]
    all_to_all x4 -> x0, waiting for transfers between devices: 160 us -> none  [the longest x1 63.3 us: per_device(): lax.all_to_all(pack_rows(incoming), 'expert', split_axis=0, concat_axis=0...]
    gather x4 -> x0, local copies, waits for them, and re-layouts: 41.3 us -> none  [the longest x2 16.8 us: pack_rows(): return padded[token_index].reshape(expert_count, capacity, width_model)]
    dot_general x5 -> x0, matrix products: 31.8 us -> none  [the longest x1 7.49 us: expert_rows(): jnp.dot(up_grad, w_up.T, preferred_element_type=jnp.float32)]
    all_to_all x4 -> x0, starting transfers between devices: 21.7 us -> none  [the longest x1 6.18 us: per_device(): lax.all_to_all(sent_inputs, 'expert', split_axis=0, concat_axis=0, tiled=...]
    ppermute x1 -> x0, waiting for transfers between devices: 19.3 us -> none  [from_behind(): lax.ppermute(shard, axis, [(i, (i + by) % size) for i in range(size)])]
    reduce_sum x2 -> x1, other arithmetic: 9.35 us -> 1.39 us  [per_device(): jnp.sum(jnp.where(picks[:, :, None] == lane, dots[:, None, :], 0.0), axis=2)]
    concatenate x3 -> x0, local copies, waits for them, and re-layouts: 7.1 us -> none  [the longest x1 4.02 us: per_device(): jnp.concatenate([returned_rows.reshape(slots_all, width_model), jnp.zeros...]
  transfers between devices with their start and end apart: 5 -> 0, of which waited for: 4 -> 0; matrix products, arithmetic and copies ran while one was open for 12% -> 0% of each run, Pallas kernels for 0% -> 0%
where the time goes in v1:
time: 231 us; the launch traced here: 230 us
  Pallas kernels  223 us (97%)
  matrix products  3.12 us (1%)
  other arithmetic  2.87 us (1%)
    pallas_call x1, Pallas kernels, exchange(): pl.pallas_call(functools.partial(kernel, sections, experts, cap), out_sha...  223 us

profile of v1, /device:TPU:18, one launch (start us, length us, event | category | flops | bytes accessed | tf_op | source)
XLA Modules:
  0.0 230.2 jit_solution(14331792837970767097)
XLA Ops:
  0.6 0.0 copy-start
  0.6 0.8 fusion.5
  1.4 0.8 copy.19
  2.2 0.0 copy-start.1
  2.2 0.0 copy-start.2
  2.2 222.6 %shard_map.95 = (f32[192,2048]{1,0:T(8,128)}, f32[192,128]{1,0:T(8,128)}) custom-call(bf16[192,2048]{1,0:T(8,128)(2,1)} %bitcast.37, bf16[192,2048]{1,0:T(8,128)(2,1)} %bitcast.38, s32[8,192]{1,0:T(8,128)} %bitcast.32, f32[8,192]{1,0:T(8,128)} %bitcast.30, bf16[2048,768]{1,0:T(8,128)(2,1)} %bitcast.34, bf16[2048,768]{1,0:T(8,128)(2,1)} %bitcast.35, ...), custom_call_target="tpu_custom_call" | custom-call | flops 12079595520 | bytes 9437184 | tf_op jit(solution)/shard_map/pallas_call | solution.py:406
  224.9 1.4 select_reduce_fusion
  226.3 0.1 copy.21
  226.3 0.0 copy-done.1
  226.4 0.6 fusion.3
  227.0 0.0 copy-done.2
  227.0 0.1 select_reduce_fusion.1
  227.1 0.0 copy-done
  227.1 3.1 %fusion.1 = bf16[1,192,2048]{2,1,0:T(8,128)(2,1)} fusion(f32[192,2048]{1,0:T(8,128)} %get-tuple-element.4, f32[192,64]{0,1:T(8,128)S(1)} %select_reduce_fusion.1, bf16[1,2048,64]{1,2,0:T(8,128)(2,1)S(1)} %copy-done), kind=kOutput, calls=%fused_computation.2 | convolution fusion | flops 302776320 | bytes 2670592 | tf_op jit(solution)/shard_map/dot_general | solution.py:472
  (2 shorter events, 0.0 us)
Async XLA Ops:
  0.6 226.4 %copy-start = (bf16[1,2048,64]{1,2,0:T(8,128)(2,1)S(1)}, bf16[1,2048,64]{1,2,0:T(8,128)(2,1)}, u32[]{:S(2)}) copy-start(bf16[1,2048,64]{1,2,0:T(8,128)(2,1)} %param.15) | copy-start | bytes 786436
  2.2 224.1 %copy-start.1 = (f32[1,192,8]{1,2,0:T(8,128)S(1)}, f32[1,192,8]{1,2,0:T(8,128)}, u32[]{:S(2)}) copy-start(f32[1,192,8]{1,2,0:T(8,128)} %param.11) | copy-start | bytes 18436
  2.2 224.8 %copy-start.2 = (s32[1,192,8]{1,2,0:T(8,128)S(1)}, s32[1,192,8]{1,2,0:T(8,128)}, u32[]{:S(2)}) copy-start(s32[1,192,8]{1,2,0:T(8,128)} %param.10) | copy-start | bytes 18436

commit v2 on v1

--- a/solution.py
+++ b/solution.py
@@ -26,7 +26,7 @@
     sections, experts, cap,
     x_ref, grad_ref, routes_ref, logits_ref, gate_ref, up_ref, down_ref,
     total_ref, dots_ref,
-    both, pack, rows, ret, back, part, fold, fold_in, meta, w_gate, w_up, w_down,
+    both, pack, rows, ret, back, part, fold, fold_in, meta, gate_act, up_act, w_gate, w_up, w_down,
     x_local, w_sem, own_send, line_send, line_recv, meta_send, meta_recv,
     pack_send, pack_recv, ret_send, ret_recv, fold_send, fold_recv, perm_sem,
 ):
@@ -175,15 +175,20 @@
             device_id=at(p, (q + group - step) % group), device_id_type=MESH,
         )
 
-    def do_expert(origin):
-        for kind in range(2):
-            for step in range(1, group):
-                pack_wait(kind, origin, step).wait_recv()
+    def do_front(origin):
+        for step in range(1, group):
+            pack_wait(0, origin, step).wait_recv()
         inputs = rows[0, origin].reshape(group * cap, width)
+        gate_act[origin] = jnp.dot(inputs, w_gate[...], preferred_element_type=F32)
+        up_act[origin] = jnp.dot(inputs, w_up[...], preferred_element_type=F32)
+
+    def do_back(origin):
+        for step in range(1, group):
+            pack_wait(1, origin, step).wait_recv()
         grads = rows[1, origin].reshape(group * cap, width)
-        pre_gate = jnp.dot(inputs, w_gate[...], preferred_element_type=F32)
-        pre_up = jnp.dot(inputs, w_up[...], preferred_element_type=F32)
         hidden = dot_nt(grads, w_down[...])
+        pre_gate = gate_act[origin]
+        pre_up = up_act[origin]
         sigmoid = jax.nn.sigmoid(pre_gate)
         active = pre_gate * sigmoid
         up_grad = hidden * active
@@ -264,11 +269,14 @@
     def candidate(n, i):
         valid_up, kind_up, origin_up = arrival(0, i)
         valid_down, kind_down, origin_down = arrival(1, i)
-        valid = jnp.where(n == 0, jnp.where(i == 0, 1, 0), jnp.where(
+        own = (i == 0) | (i == -1)
+        valid = jnp.where(n == 0, jnp.where(own, 1, 0), jnp.where(
             n == 1, jnp.where(valid_up, 1, 0), jnp.where(valid_down, 1, 0)))
-        kind = jnp.where(n == 0, 1, jnp.where(n == 1, kind_up, kind_down))
+        kind = jnp.where(n == 0, i + 1, jnp.where(n == 1, kind_up, kind_down))
         origin = jnp.where(n == 0, p, jnp.where(n == 1, origin_up, origin_down))
         return valid == 1, kind, origin
+
+    late = jnp.where((p == 0) | (p == LINE - 1), 0, 1)
 
     def turn(i, carry):
         for way in range(2):
@@ -306,20 +314,35 @@
             def _():
                 do_combine(origin)
 
-        def expert_one(valid, kind, origin):
+        def front_one(valid, kind, origin):
+            @pl.when(valid & (kind == 0))
+            def _():
+                do_front(origin)
+
+        def back_one(valid, kind, origin):
             @pl.when(valid & (kind == 1))
             def _():
-                do_expert(origin)
+                do_back(origin)
 
         each(i, pack_one)
-        each(i - 1, combine_one)
 
         @pl.when(i == 0)
         def _():
             for copy in weights:
                 copy.wait()
 
-        each(i, expert_one)
+        each(i - 1, front_one)
+
+        @pl.when(late == 0)
+        def _():
+            each(i - 1, combine_one)
+
+        each(i - late, back_one)
+
+        @pl.when(late == 1)
+        def _():
+            each(i - 2, combine_one)
+
         return carry
 
     lax.fori_loop(0, 2 * LINE - 1, turn, 0)
@@ -421,6 +444,8 @@
             pltpu.VMEM((LINE, tokens, wide), BF16),
             pltpu.VMEM((LINE + 1, tokens, wide), BF16),
             pltpu.VMEM((LINE, 2, experts, tokens), F32),
+            pltpu.VMEM((LINE, group * cap, hidden), F32),
+            pltpu.VMEM((LINE, group * cap, hidden), F32),
             pltpu.VMEM((width, hidden), BF16),
             pltpu.VMEM((width, hidden), BF16),
             pltpu.VMEM((hidden, width), BF16),

time: 231 us -> 197 us (0.85)
  Pallas kernels: 223 us -> 189 us
    pallas_call x1, Pallas kernels: 223 us -> 189 us  [exchange(): pl.pallas_call(functools.partial(kernel, sections, experts, cap), out_sha...]
where the time goes in v2:
time: 197 us
  Pallas kernels  189 us (96%)
  matrix products  3.13 us (2%)
  other arithmetic  2.87 us (1%)
    pallas_call x1, Pallas kernels, exchange(): pl.pallas_call(functools.partial(kernel, sections, experts, cap), out_sha...  189 us

profile of v2, /device:TPU:18, one launch (start us, length us, event | category | flops | bytes accessed | tf_op | source)
XLA Modules:
  0.0 197.0 jit_solution(17818075617022694403)
XLA Ops:
  0.6 0.0 copy-start
  0.6 0.8 fusion.5
  1.4 0.8 copy.19
  2.2 0.0 copy-start.1
  2.2 0.0 copy-start.2
  2.2 189.4 %shard_map.95 = (f32[192,2048]{1,0:T(8,128)}, f32[192,128]{1,0:T(8,128)}) custom-call(bf16[192,2048]{1,0:T(8,128)(2,1)} %bitcast.37, bf16[192,2048]{1,0:T(8,128)(2,1)} %bitcast.38, s32[8,192]{1,0:T(8,128)} %bitcast.32, f32[8,192]{1,0:T(8,128)} %bitcast.30, bf16[2048,768]{1,0:T(8,128)(2,1)} %bitcast.34, bf16[2048,768]{1,0:T(8,128)(2,1)} %bitcast.35, ...), custom_call_target="tpu_custom_call" | custom-call | flops 12079595520 | bytes 9437184 | tf_op jit(solution)/shard_map/pallas_call | solution.py:429
  191.6 1.4 select_reduce_fusion
  193.0 0.1 copy.21
  193.1 0.0 copy-done.1
  193.1 0.6 fusion.3
  193.8 0.0 copy-done.2
  193.8 0.1 select_reduce_fusion.1
  193.8 0.0 copy-done
  193.9 3.1 %fusion.1 = bf16[1,192,2048]{2,1,0:T(8,128)(2,1)} fusion(f32[192,2048]{1,0:T(8,128)} %get-tuple-element.4, f32[192,64]{0,1:T(8,128)S(1)} %select_reduce_fusion.1, bf16[1,2048,64]{1,2,0:T(8,128)(2,1)S(1)} %copy-done), kind=kOutput, calls=%fused_computation.2 | convolution fusion | flops 302776320 | bytes 2670592 | tf_op jit(solution)/shard_map/dot_general | solution.py:497
  (2 shorter events, 0.0 us)
Async XLA Ops:
  0.6 193.2 %copy-start = (bf16[1,2048,64]{1,2,0:T(8,128)(2,1)S(1)}, bf16[1,2048,64]{1,2,0:T(8,128)(2,1)}, u32[]{:S(2)}) copy-start(bf16[1,2048,64]{1,2,0:T(8,128)(2,1)} %param.15) | copy-start | bytes 786436
  2.2 190.9 %copy-start.1 = (f32[1,192,8]{1,2,0:T(8,128)S(1)}, f32[1,192,8]{1,2,0:T(8,128)}, u32[]{:S(2)}) copy-start(f32[1,192,8]{1,2,0:T(8,128)} %param.11) | copy-start | bytes 18436
  2.2 191.5 %copy-start.2 = (s32[1,192,8]{1,2,0:T(8,128)S(1)}, s32[1,192,8]{1,2,0:T(8,128)}, u32[]{:S(2)}) copy-start(s32[1,192,8]{1,2,0:T(8,128)} %param.10) | copy-start | bytes 18436

commit v3 on v2

--- a/solution.py
+++ b/solution.py
@@ -10,6 +10,7 @@
 MESH = pl.DeviceIdType.MESH
 LINE = 4
 LANES = 128
+PIECES = 2
 F32 = jnp.float32
 BF16 = jnp.bfloat16
 
@@ -38,6 +39,14 @@
     p = me // group
     q = me % group
     far = LINE - 1 - p
+    part_width = width // PIECES
+
+    def cut(piece):
+        return pl.ds(piece * part_width, part_width)
+
+    def cut_wide(piece):
+        return pl.ds(piece * part_width, part_width + (LANES if piece == PIECES - 1 else 0))
+
     before = (section + sections - 1) % sections
     after = (section + 1) % sections
 
@@ -59,32 +68,39 @@
     keep_x.start()
     pl.semaphore_wait(barrier, LINE + group)
 
-    def own_x(way):
-        return pltpu.make_async_remote_copy(
-            src_ref=x_ref, dst_ref=both.at[0, p], send_sem=own_send.at[way],
-            recv_sem=line_recv.at[0, p], device_id=at((p + (1, LINE - 1)[way]) % LINE, q),
+    def own_x(way, piece):
+        return pltpu.make_async_remote_copy(
+            src_ref=x_ref.at[:, cut(piece)], dst_ref=both.at[0, p, :, cut(piece)],
+            send_sem=own_send.at[way, piece],
+            recv_sem=line_recv.at[0, p, piece], device_id=at((p + (1, LINE - 1)[way]) % LINE, q),
             device_id_type=MESH,
         )
 
-    def line_copy(kind, origin, way):
-        return pltpu.make_async_remote_copy(
-            src_ref=both.at[kind, origin], dst_ref=both.at[kind, origin],
-            send_sem=line_send.at[kind, origin, way], recv_sem=line_recv.at[kind, origin],
+    def line_copy(kind, origin, way, piece):
+        return pltpu.make_async_remote_copy(
+            src_ref=both.at[kind, origin, :, cut(piece)],
+            dst_ref=both.at[kind, origin, :, cut(piece)],
+            send_sem=line_send.at[kind, origin, way, piece],
+            recv_sem=line_recv.at[kind, origin, piece],
             device_id=at((p + (1, LINE - 1)[way]) % LINE, q), device_id_type=MESH,
         )
 
     def has(way):
         return (p < LINE - 1) if way == 0 else (p > 0)
 
-    for way in range(2):
-        @pl.when(has(way))
-        def _():
-            own_x(way).start()
-    permute = pltpu.make_async_remote_copy(
-        src_ref=grad_ref, dst_ref=both.at[1, p], send_sem=perm_sem.at[0], recv_sem=perm_sem.at[1],
-        device_id=(before, me), device_id_type=MESH,
-    )
-    permute.start()
+    def permute(piece):
+        return pltpu.make_async_remote_copy(
+            src_ref=grad_ref.at[:, cut(piece)], dst_ref=both.at[1, p, :, cut(piece)],
+            send_sem=perm_sem.at[0, piece], recv_sem=perm_sem.at[1, piece],
+            device_id=(before, me), device_id_type=MESH,
+        )
+
+    for piece in range(PIECES):
+        for way in range(2):
+            @pl.when(has(way))
+            def _():
+                own_x(way, piece).start()
+        permute(piece).start()
 
     routes = routes_ref[...]
     exponent = jnp.exp(logits_ref[...])
@@ -130,63 +146,67 @@
 
     place = lax.broadcasted_iota(jnp.int32, (cap, tokens), 0).astype(F32)
 
-    def pack_copy(kind, origin, step):
-        return pltpu.make_async_remote_copy(
-            src_ref=pack.at[kind, origin, step - 1],
-            dst_ref=rows.at[kind, origin, q],
-            send_sem=pack_send.at[kind, origin, step],
-            recv_sem=pack_recv.at[kind, origin, step],
+    def pack_copy(kind, origin, step, piece):
+        return pltpu.make_async_remote_copy(
+            src_ref=pack.at[kind, origin, step - 1, :, cut(piece)],
+            dst_ref=rows.at[kind, origin, q, :, cut(piece)],
+            send_sem=pack_send.at[kind, origin, step, piece],
+            recv_sem=pack_recv.at[kind, origin, step, piece],
             device_id=at(p, (q + step) % group), device_id_type=MESH,
         )
 
-    def pack_wait(kind, origin, step):
-        return pltpu.make_async_remote_copy(
-            src_ref=pack.at[kind, origin, step - 1],
-            dst_ref=rows.at[kind, origin, (q + group - step) % group],
-            send_sem=pack_send.at[kind, origin, step],
-            recv_sem=pack_recv.at[kind, origin, step],
+    def pack_wait(kind, origin, step, piece):
+        return pltpu.make_async_remote_copy(
+            src_ref=pack.at[kind, origin, step - 1, :, cut(piece)],
+            dst_ref=rows.at[kind, origin, (q + group - step) % group, :, cut(piece)],
+            send_sem=pack_send.at[kind, origin, step, piece],
+            recv_sem=pack_recv.at[kind, origin, step, piece],
             device_id=at(p, (q + step) % group), device_id_type=MESH,
         )
 
-    def do_pack(kind, origin):
-        source = both[kind, origin]
+    def do_pack(kind, origin, piece):
+        source = both[kind, origin, :, cut(piece)]
         for step in list(range(1, group)) + [0]:
             pick = jnp.where(chosen(origin, 0, (q + step) % group) == place, 1.0, 0.0).astype(BF16)
             packed = jnp.dot(pick, source, preferred_element_type=F32).astype(BF16)
             if step == 0:
-                rows[kind, origin, q] = packed
+                rows[kind, origin, q, :, cut(piece)] = packed
             else:
-                pack[kind, origin, step - 1] = packed
-                pack_copy(kind, origin, step).start()
-
-    def ret_copy(origin, step):
+                pack[kind, origin, step - 1, :, cut(piece)] = packed
+                pack_copy(kind, origin, step, piece).start()
+
+    def ret_copy(origin, step, piece):
         slot = (q + group - step) % group
         return pltpu.make_async_remote_copy(
-            src_ref=ret.at[origin, slot], dst_ref=back.at[origin, q],
-            send_sem=ret_send.at[origin, step], recv_sem=ret_recv.at[origin, step],
+            src_ref=ret.at[origin, slot, :, cut_wide(piece)],
+            dst_ref=back.at[origin, q, :, cut_wide(piece)],
+            send_sem=ret_send.at[origin, step, piece], recv_sem=ret_recv.at[origin, step, piece],
             device_id=at(p, slot), device_id_type=MESH,
         )
 
-    def ret_wait(origin, step):
-        return pltpu.make_async_remote_copy(
-            src_ref=ret.at[origin, (q + group - step) % group],
-            dst_ref=back.at[origin, (q + step) % group],
-            send_sem=ret_send.at[origin, step], recv_sem=ret_recv.at[origin, step],
+    def ret_wait(origin, step, piece):
+        return pltpu.make_async_remote_copy(
+            src_ref=ret.at[origin, (q + group - step) % group, :, cut_wide(piece)],
+            dst_ref=back.at[origin, (q + step) % group, :, cut_wide(piece)],
+            send_sem=ret_send.at[origin, step, piece], recv_sem=ret_recv.at[origin, step, piece],
             device_id=at(p, (q + group - step) % group), device_id_type=MESH,
         )
 
     def do_front(origin):
-        for step in range(1, group):
-            pack_wait(0, origin, step).wait_recv()
+        for piece in range(PIECES):
+            for step in range(1, group):
+                pack_wait(0, origin, step, piece).wait_recv()
         inputs = rows[0, origin].reshape(group * cap, width)
         gate_act[origin] = jnp.dot(inputs, w_gate[...], preferred_element_type=F32)
         up_act[origin] = jnp.dot(inputs, w_up[...], preferred_element_type=F32)
 
     def do_back(origin):
-        for step in range(1, group):
-            pack_wait(1, origin, step).wait_recv()
-        grads = rows[1, origin].reshape(group * cap, width)
-        hidden = dot_nt(grads, w_down[...])
+        hidden = jnp.zeros((group * cap, w_down.shape[0]), F32)
+        for piece in range(PIECES):
+            for step in range(1, group):
+                pack_wait(1, origin, step, piece).wait_recv()
+            grads = rows[1, origin, :, :, cut(piece)].reshape(group * cap, part_width)
+            hidden = hidden + dot_nt(grads, w_down[:, cut(piece)])
         pre_gate = gate_act[origin]
         pre_up = up_act[origin]
         sigmoid = jax.nn.sigmoid(pre_gate)
@@ -194,38 +214,40 @@
         up_grad = hidden * active
         dots = jnp.sum(up_grad * pre_up, axis=1, keepdims=True)
         gate_grad = hidden * pre_up * sigmoid * (1.0 + pre_gate * (1.0 - sigmoid))
-        pair = dot_nt(gate_grad.astype(BF16), w_gate[...]) + dot_nt(up_grad.astype(BF16), w_up[...])
+        gate_grad = gate_grad.astype(BF16)
+        up_grad = up_grad.astype(BF16)
         lane = lax.broadcasted_iota(jnp.int32, (group * cap, LANES), 1)
-        ret[origin, :, :, :width] = pair.astype(BF16).reshape(group, cap, width)
         ret[origin, :, :, width:] = (
             jnp.where(lane == me, dots, 0.0).astype(BF16).reshape(group, cap, LANES)
         )
-        for step in range(1, group):
-            ret_copy(origin, step).start()
+        for piece in range(PIECES):
+            pair = dot_nt(gate_grad, w_gate[cut(piece), :]) + dot_nt(up_grad, w_up[cut(piece), :])
+            ret[origin, :, :, cut(piece)] = pair.astype(BF16).reshape(group, cap, part_width)
+            for step in range(1, group):
+                ret_copy(origin, step, piece).start()
         back[origin, q] = ret[origin, q]
 
-    def fold_copy(origin, way):
+    def fold_copy(origin, way, piece):
         target = p + 1 - 2 * way
         if way == 0:
             slot = jnp.where(origin == target, LINE, origin)
         else:
             slot = origin
         return pltpu.make_async_remote_copy(
-            src_ref=fold.at[origin], dst_ref=fold_in.at[slot],
-            send_sem=fold_send.at[origin], recv_sem=fold_recv.at[slot],
+            src_ref=fold.at[origin, :, cut_wide(piece)],
+            dst_ref=fold_in.at[slot, :, cut_wide(piece)],
+            send_sem=fold_send.at[origin, piece], recv_sem=fold_recv.at[slot, piece],
             device_id=at((p + (1, LINE - 1)[way]) % LINE, q), device_id_type=MESH,
         )
 
-    def fold_wait(slot):
-        return pltpu.make_async_remote_copy(
-            src_ref=fold.at[0], dst_ref=fold_in.at[slot],
-            send_sem=fold_send.at[0], recv_sem=fold_recv.at[slot],
+    def fold_wait(slot, piece):
+        return pltpu.make_async_remote_copy(
+            src_ref=fold.at[0, :, cut_wide(piece)], dst_ref=fold_in.at[slot, :, cut_wide(piece)],
+            send_sem=fold_send.at[0, piece], recv_sem=fold_recv.at[slot, piece],
             device_id=at((p + 1) % LINE, q), device_id_type=MESH,
         )
 
     def do_combine(origin):
-        for step in range(1, group):
-            ret_wait(origin, step).wait_recv()
         picks, highs, lows = [], [], []
         for slot in range(group):
             hit = chosen(origin, 0, slot) == place
@@ -235,26 +257,30 @@
             highs.append(high)
             lows.append((weigh - high.astype(F32)).astype(BF16))
         pick, high, low = (jnp.concatenate(parts, axis=0) for parts in (picks, highs, lows))
-        came = back[origin, :, :, :width].reshape(group * cap, width)
-        marks = back[origin, :, :, width:].reshape(group * cap, LANES)
-        part[origin, :, :width] = dot_tn(high, came) + dot_tn(low, came)
-        part[origin, :, width:] = dot_tn(pick, marks)
-
-        @pl.when((p == LINE - 1) & (origin < p))
-        def _():
-            fold[origin] = part[origin].astype(BF16)
-            fold_copy(origin, 1).start()
-
-        @pl.when((p == 0) & (origin > p))
-        def _():
-            fold[origin] = part[origin].astype(BF16)
-            fold_copy(origin, 0).start()
+        for piece in range(PIECES):
+            for step in range(1, group):
+                ret_wait(origin, step, piece).wait_recv()
+            came = back[origin, :, :, cut(piece)].reshape(group * cap, part_width)
+            part[origin, :, cut(piece)] = dot_tn(high, came) + dot_tn(low, came)
+            if piece == PIECES - 1:
+                marks = back[origin, :, :, width:].reshape(group * cap, LANES)
+                part[origin, :, width:] = dot_tn(pick, marks)
+
+            @pl.when((p == LINE - 1) & (origin < p))
+            def _():
+                fold[origin, :, cut_wide(piece)] = part[origin, :, cut_wide(piece)].astype(BF16)
+                fold_copy(origin, 1, piece).start()
+
+            @pl.when((p == 0) & (origin > p))
+            def _():
+                fold[origin, :, cut_wide(piece)] = part[origin, :, cut_wide(piece)].astype(BF16)
+                fold_copy(origin, 0, piece).start()
 
     keep_x.wait()
-    do_pack(0, p)
+    for piece in range(PIECES):
+        do_pack(0, p, piece)
     for step in range(1, LINE):
         meta_wait(step).wait_recv()
-    permute.wait_recv()
 
     def arrival(way, i):
         count = p if way == 0 else far
@@ -279,22 +305,30 @@
     late = jnp.where((p == 0) | (p == LINE - 1), 0, 1)
 
     def turn(i, carry):
-        for way in range(2):
-            valid, kind, origin = arrival(way, i)
-
-            @pl.when(valid)
-            def _():
-                line_copy(kind, origin, way).wait_recv()
-
-                @pl.when(has(way))
-                def _():
-                    line_copy(kind, origin, way).start()
-
-            count = p if way == 0 else far
-
-            @pl.when((i == 2 * count) & has(way))
-            def _():
-                line_copy(1, p, way).start()
+        def forward(piece):
+            @pl.when(i == 0)
+            def _():
+                permute(piece).wait_recv()
+
+            for way in range(2):
+                valid, kind, origin = arrival(way, i)
+
+                @pl.when(valid)
+                def _():
+                    line_copy(kind, origin, way, piece).wait_recv()
+
+                    @pl.when(has(way))
+                    def _():
+                        line_copy(kind, origin, way, piece).start()
+
+        def own_gradients():
+            for way in range(2):
+                count = p if way == 0 else far
+
+                @pl.when((i == jnp.maximum(2 * count - 1, 0)) & has(way))
+                def _():
+                    for piece in range(PIECES):
+                        line_copy(1, p, way, piece).start()
 
         def each(step, body):
             def one(n, carry):
@@ -304,10 +338,10 @@
 
             lax.fori_loop(0, 3, one, 0)
 
-        def pack_one(valid, kind, origin):
+        def pack_one(piece, valid, kind, origin):
             @pl.when(valid)
             def _():
-                do_pack(kind, origin)
+                do_pack(kind, origin, piece)
 
         def combine_one(valid, kind, origin):
             @pl.when(valid & (kind == 1))
@@ -324,7 +358,11 @@
             def _():
                 do_back(origin)
 
-        each(i, pack_one)
+        for piece in range(PIECES):
+            forward(piece)
+            if piece == PIECES - 1:
+                own_gradients()
+            each(i, functools.partial(pack_one, piece))
 
         @pl.when(i == 0)
         def _():
@@ -348,28 +386,38 @@
     lax.fori_loop(0, 2 * LINE - 1, turn, 0)
 
     def gather_back(r, carry):
-        @pl.when((p < LINE - 1) & (r <= p))
-        def _():
-            fold_wait(r).wait_recv()
-            part[r] = part[r] + fold_in[r].astype(F32)
-
-            @pl.when(r < p)
-            def _():
-                fold[r] = part[r].astype(BF16)
-                fold_copy(r, 1).start()
-
         origin = LINE - 1 - r
-
-        @pl.when((p > 0) & (origin >= p))
-        def _():
-            slot = jnp.where(origin == p, LINE, origin)
-            fold_wait(slot).wait_recv()
-            part[origin] = part[origin] + fold_in[slot].astype(F32)
-
-            @pl.when(origin > p)
-            def _():
-                fold[origin] = part[origin].astype(BF16)
-                fold_copy(origin, 0).start()
+        slot = jnp.where(origin == p, LINE, origin)
+        for piece in range(PIECES):
+            where = cut_wide(piece)
+
+            @pl.when((p < LINE - 1) & (r <= p))
+            def _():
+                fold_wait(r, piece).wait_recv()
+                summed = part[r, :, where] + fold_in[r, :, where].astype(F32)
+
+                @pl.when(r < p)
+                def _():
+                    fold[r, :, where] = summed.astype(BF16)
+                    fold_copy(r, 1, piece).start()
+
+                @pl.when(r == p)
+                def _():
+                    part[r, :, where] = summed
+
+            @pl.when((p > 0) & (origin >= p))
+            def _():
+                fold_wait(slot, piece).wait_recv()
+                summed = part[origin, :, where] + fold_in[slot, :, where].astype(F32)
+
+                @pl.when(origin > p)
+                def _():
+                    fold[origin, :, where] = summed.astype(BF16)
+                    fold_copy(origin, 0, piece).start()
+
+                @pl.when(origin == p)
+                def _():
+                    part[origin, :, where] = summed
 
         return carry
 
@@ -377,38 +425,40 @@
     total_ref[...] = part[p, :, :width] + both[1, p].astype(F32)
     dots_ref[...] = part[p, :, width:]
 
-    permute.wait_send()
     for step in range(1, LINE):
         meta_copy(step).wait_send()
-    for way in range(2):
-        @pl.when(has(way))
-        def _():
-            own_x(way).wait_send()
-            line_copy(1, p, way).wait_send()
+    for piece in range(PIECES):
+        permute(piece).wait_send()
+        for way in range(2):
+            @pl.when(has(way))
+            def _():
+                own_x(way, piece).wait_send()
+                line_copy(1, p, way, piece).wait_send()
 
     def finish(origin, carry):
-        for kind in range(2):
+        for piece in range(PIECES):
+            for kind in range(2):
+                for step in range(1, group):
+                    pack_copy(kind, origin, step, piece).wait_send()
+
+                @pl.when((origin < p) & has(0))
+                def _():
+                    line_copy(kind, origin, 0, piece).wait_send()
+
+                @pl.when((origin > p) & has(1))
+                def _():
+                    line_copy(kind, origin, 1, piece).wait_send()
+
             for step in range(1, group):
-                pack_copy(kind, origin, step).wait_send()
-
-            @pl.when((origin < p) & has(0))
-            def _():
-                line_copy(kind, origin, 0).wait_send()
-
-            @pl.when((origin > p) & has(1))
-            def _():
-                line_copy(kind, origin, 1).wait_send()
-
-        for step in range(1, group):
-            ret_copy(origin, step).wait_send()
-
-        @pl.when(origin < p)
-        def _():
-            fold_copy(origin, 1).wait_send()
-
-        @pl.when(origin > p)
-        def _():
-            fold_copy(origin, 0).wait_send()
+                ret_copy(origin, step, piece).wait_send()
+
+            @pl.when(origin < p)
+            def _():
+                fold_copy(origin, 1, piece).wait_send()
+
+            @pl.when(origin > p)
+            def _():
+                fold_copy(origin, 0, piece).wait_send()
 
         return carry
 
@@ -451,18 +501,18 @@
             pltpu.VMEM((hidden, width), BF16),
             dma(()),
             dma((3,)),
-            dma((2,)),
-            dma((2, LINE, 2)),
-            dma((2, LINE)),
+            dma((2, PIECES)),
+            dma((2, LINE, 2, PIECES)),
+            dma((2, LINE, PIECES)),
             dma((LINE,)),
             dma((LINE,)),
-            dma((2, LINE, group)),
-            dma((2, LINE, group)),
-            dma((LINE, group)),
-            dma((LINE, group)),
-            dma((LINE,)),
-            dma((LINE + 1,)),
-            dma((2,)),
+            dma((2, LINE, group, PIECES)),
+            dma((2, LINE, group, PIECES)),
+            dma((LINE, group, PIECES)),
+            dma((LINE, group, PIECES)),
+            dma((LINE, PIECES)),
+            dma((LINE + 1, PIECES)),
+            dma((2, PIECES)),
         ],
         compiler_params=pltpu.CompilerParams(
             collective_id=0, has_side_effects=True, vmem_limit_bytes=63 * 1024 * 1024

time: 197 us -> 199 us (1.010)
  Pallas kernels: 189 us -> 191 us
where the time goes in v3:
time: 199 us
  Pallas kernels  191 us (96%)
  matrix products  3.12 us (2%)
  other arithmetic  2.87 us (1%)
    pallas_call x1, Pallas kernels, exchange(): pl.pallas_call(functools.partial(kernel, sections, experts, cap), out_sha...  191 us

profile of v3, /device:TPU:18, one launch (start us, length us, event | category | flops | bytes accessed | tf_op | source)
XLA Modules:
  0.0 198.7 jit_solution(13372286496508154519)
XLA Ops:
  0.6 0.0 copy-start
  0.6 0.8 fusion.5
  1.4 0.8 copy.19
  2.2 0.0 copy-start.1
  2.2 0.0 copy-start.2
  2.2 191.1 %shard_map.95 = (f32[192,2048]{1,0:T(8,128)}, f32[192,128]{1,0:T(8,128)}) custom-call(bf16[192,2048]{1,0:T(8,128)(2,1)} %bitcast.37, bf16[192,2048]{1,0:T(8,128)(2,1)} %bitcast.38, s32[8,192]{1,0:T(8,128)} %bitcast.32, f32[8,192]{1,0:T(8,128)} %bitcast.30, bf16[2048,768]{1,0:T(8,128)(2,1)} %bitcast.34, bf16[2048,768]{1,0:T(8,128)(2,1)} %bitcast.35, ...), custom_call_target="tpu_custom_call" | custom-call | flops 12079595520 | bytes 9437184 | tf_op jit(solution)/shard_map/pallas_call | solution.py:479
  193.4 1.4 select_reduce_fusion
  194.8 0.1 copy.21
  194.8 0.0 copy-done.1
  194.9 0.6 fusion.3
  195.5 0.0 copy-done.2
  195.5 0.1 select_reduce_fusion.1
  195.6 0.0 copy-done
  195.6 3.1 %fusion.1 = bf16[1,192,2048]{2,1,0:T(8,128)(2,1)} fusion(f32[192,2048]{1,0:T(8,128)} %get-tuple-element.4, f32[192,64]{0,1:T(8,128)S(1)} %select_reduce_fusion.1, bf16[1,2048,64]{1,2,0:T(8,128)(2,1)S(1)} %copy-done), kind=kOutput, calls=%fused_computation.2 | convolution fusion | flops 302776320 | bytes 2670592 | tf_op jit(solution)/shard_map/dot_general | solution.py:547
  (2 shorter events, 0.0 us)
Async XLA Ops:
  0.6 195.0 %copy-start = (bf16[1,2048,64]{1,2,0:T(8,128)(2,1)S(1)}, bf16[1,2048,64]{1,2,0:T(8,128)(2,1)}, u32[]{:S(2)}) copy-start(bf16[1,2048,64]{1,2,0:T(8,128)(2,1)} %param.15) | copy-start | bytes 786436
  2.2 192.6 %copy-start.1 = (f32[1,192,8]{1,2,0:T(8,128)S(1)}, f32[1,192,8]{1,2,0:T(8,128)}, u32[]{:S(2)}) copy-start(f32[1,192,8]{1,2,0:T(8,128)} %param.11) | copy-start | bytes 18436
  2.2 193.3 %copy-start.2 = (s32[1,192,8]{1,2,0:T(8,128)S(1)}, s32[1,192,8]{1,2,0:T(8,128)}, u32[]{:S(2)}) copy-start(s32[1,192,8]{1,2,0:T(8,128)} %param.10) | copy-start | bytes 18436

commit v4 on v3

--- a/solution.py
+++ b/solution.py
@@ -17,10 +17,6 @@
 
 def dot_nt(a, b):
     return lax.dot_general(a, b, (((1,), (1,)), ((), ())), preferred_element_type=F32)
-
-
-def dot_tn(a, b):
-    return lax.dot_general(a, b, (((0,), (0,)), ((), ())), preferred_element_type=F32)
 
 
 def kernel(
@@ -197,32 +193,33 @@
             for step in range(1, group):
                 pack_wait(0, origin, step, piece).wait_recv()
         inputs = rows[0, origin].reshape(group * cap, width)
-        gate_act[origin] = jnp.dot(inputs, w_gate[...], preferred_element_type=F32)
-        up_act[origin] = jnp.dot(inputs, w_up[...], preferred_element_type=F32)
+        gate_act[origin] = jnp.dot(inputs, w_gate[...], preferred_element_type=F32).T
+        up_act[origin] = jnp.dot(inputs, w_up[...], preferred_element_type=F32).T
 
     def do_back(origin):
-        hidden = jnp.zeros((group * cap, w_down.shape[0]), F32)
+        hidden = jnp.zeros((w_down.shape[0], group * cap), F32)
         for piece in range(PIECES):
             for step in range(1, group):
                 pack_wait(1, origin, step, piece).wait_recv()
             grads = rows[1, origin, :, :, cut(piece)].reshape(group * cap, part_width)
-            hidden = hidden + dot_nt(grads, w_down[:, cut(piece)])
+            hidden = hidden + dot_nt(w_down[:, cut(piece)], grads)
         pre_gate = gate_act[origin]
         pre_up = up_act[origin]
         sigmoid = jax.nn.sigmoid(pre_gate)
         active = pre_gate * sigmoid
         up_grad = hidden * active
-        dots = jnp.sum(up_grad * pre_up, axis=1, keepdims=True)
+        dots = jnp.sum(up_grad * pre_up, axis=0, keepdims=True)
         gate_grad = hidden * pre_up * sigmoid * (1.0 + pre_gate * (1.0 - sigmoid))
         gate_grad = gate_grad.astype(BF16)
         up_grad = up_grad.astype(BF16)
-        lane = lax.broadcasted_iota(jnp.int32, (group * cap, LANES), 1)
+        lane = lax.broadcasted_iota(jnp.int32, (LANES, group * cap), 0)
         ret[origin, :, :, width:] = (
-            jnp.where(lane == me, dots, 0.0).astype(BF16).reshape(group, cap, LANES)
-        )
-        for piece in range(PIECES):
-            pair = dot_nt(gate_grad, w_gate[cut(piece), :]) + dot_nt(up_grad, w_up[cut(piece), :])
-            ret[origin, :, :, cut(piece)] = pair.astype(BF16).reshape(group, cap, part_width)
+            jnp.where(lane == me, dots, 0.0).T.astype(BF16).reshape(group, cap, LANES)
+        )
+        for piece in range(PIECES):
+            pair = jnp.dot(w_gate[cut(piece), :], gate_grad, preferred_element_type=F32)
+            pair = pair + jnp.dot(w_up[cut(piece), :], up_grad, preferred_element_type=F32)
+            ret[origin, :, :, cut(piece)] = pair.T.astype(BF16).reshape(group, cap, part_width)
             for step in range(1, group):
                 ret_copy(origin, step, piece).start()
         back[origin, q] = ret[origin, q]
@@ -248,23 +245,25 @@
         )
 
     def do_combine(origin):
-        picks, highs, lows = [], [], []
+        shares = []
         for slot in range(group):
             hit = chosen(origin, 0, slot) == place
-            weigh = jnp.where(hit, chosen(origin, 1, slot), 0.0)
-            high = weigh.astype(BF16)
-            picks.append(jnp.where(hit, 1.0, 0.0).astype(BF16))
-            highs.append(high)
-            lows.append((weigh - high.astype(F32)).astype(BF16))
-        pick, high, low = (jnp.concatenate(parts, axis=0) for parts in (picks, highs, lows))
+            shares.append(jnp.where(hit, chosen(origin, 1, slot), 0.0))
+        weigh = jnp.concatenate(shares, axis=0).T
+        high = weigh.astype(BF16)
+        low = (weigh - high.astype(F32)).astype(BF16)
+        pick = jnp.where(weigh > 0.0, 1.0, 0.0).astype(BF16)
         for piece in range(PIECES):
             for step in range(1, group):
                 ret_wait(origin, step, piece).wait_recv()
             came = back[origin, :, :, cut(piece)].reshape(group * cap, part_width)
-            part[origin, :, cut(piece)] = dot_tn(high, came) + dot_tn(low, came)
+            part[origin, :, cut(piece)] = (
+                jnp.dot(high, came, preferred_element_type=F32)
+                + jnp.dot(low, came, preferred_element_type=F32)
+            )
             if piece == PIECES - 1:
                 marks = back[origin, :, :, width:].reshape(group * cap, LANES)
-                part[origin, :, width:] = dot_tn(pick, marks)
+                part[origin, :, width:] = jnp.dot(pick, marks, preferred_element_type=F32)
 
             @pl.when((p == LINE - 1) & (origin < p))
             def _():
@@ -387,41 +386,35 @@
 
     def gather_back(r, carry):
         origin = LINE - 1 - r
-        slot = jnp.where(origin == p, LINE, origin)
         for piece in range(PIECES):
             where = cut_wide(piece)
 
-            @pl.when((p < LINE - 1) & (r <= p))
+            @pl.when((p < LINE - 1) & (r < p))
             def _():
                 fold_wait(r, piece).wait_recv()
                 summed = part[r, :, where] + fold_in[r, :, where].astype(F32)
-
-                @pl.when(r < p)
-                def _():
-                    fold[r, :, where] = summed.astype(BF16)
-                    fold_copy(r, 1, piece).start()
-
-                @pl.when(r == p)
-                def _():
-                    part[r, :, where] = summed
-
-            @pl.when((p > 0) & (origin >= p))
-            def _():
+                fold[r, :, where] = summed.astype(BF16)
+                fold_copy(r, 1, piece).start()
+
+            @pl.when((p > 0) & (origin > p))
+            def _():
+                fold_wait(origin, piece).wait_recv()
+                summed = part[origin, :, where] + fold_in[origin, :, where].astype(F32)
+                fold[origin, :, where] = summed.astype(BF16)
+                fold_copy(origin, 0, piece).start()
+
+        return carry
+
+    lax.fori_loop(0, LINE - 1, gather_back, 0)
+    for piece in range(PIECES):
+        where = cut_wide(piece)
+        for way in range(2):
+            @pl.when(has(1 - way))
+            def _():
+                slot = LINE if way == 0 else p
                 fold_wait(slot, piece).wait_recv()
-                summed = part[origin, :, where] + fold_in[slot, :, where].astype(F32)
-
-                @pl.when(origin > p)
-                def _():
-                    fold[origin, :, where] = summed.astype(BF16)
-                    fold_copy(origin, 0, piece).start()
-
-                @pl.when(origin == p)
-                def _():
-                    part[origin, :, where] = summed
-
-        return carry
-
-    lax.fori_loop(0, LINE, gather_back, 0)
+                part[p, :, where] = part[p, :, where] + fold_in[slot, :, where].astype(F32)
+
     total_ref[...] = part[p, :, :width] + both[1, p].astype(F32)
     dots_ref[...] = part[p, :, width:]
 
@@ -494,8 +487,8 @@
             pltpu.VMEM((LINE, tokens, wide), BF16),
             pltpu.VMEM((LINE + 1, tokens, wide), BF16),
             pltpu.VMEM((LINE, 2, experts, tokens), F32),
-            pltpu.VMEM((LINE, group * cap, hidden), F32),
-            pltpu.VMEM((LINE, group * cap, hidden), F32),
+            pltpu.VMEM((LINE, hidden, group * cap), F32),
+            pltpu.VMEM((LINE, hidden, group * cap), F32),
             pltpu.VMEM((width, hidden), BF16),
             pltpu.VMEM((width, hidden), BF16),
             pltpu.VMEM((hidden, width), BF16),

time: 199 us -> 186 us (0.935)
  Pallas kernels: 191 us -> 179 us
    pallas_call x1, Pallas kernels: 191 us -> 179 us  [exchange(): pl.pallas_call(functools.partial(kernel, sections, experts, cap), out_sha...]
where the time goes in v4:
time: 186 us
  Pallas kernels  179 us (96%)
  matrix products  3.13 us (2%)
  other arithmetic  2.87 us (2%)
    pallas_call x1, Pallas kernels, exchange(): pl.pallas_call(functools.partial(kernel, sections, experts, cap), out_sha...  179 us

profile of v4, /device:TPU:18, one launch (start us, length us, event | category | flops | bytes accessed | tf_op | source)
XLA Modules:
  0.0 186.2 jit_solution(2584868597052598646)
XLA Ops:
  0.6 0.0 copy-start
  0.6 0.8 fusion.5
  1.4 0.8 copy.19
  2.2 0.0 copy-start.1
  2.2 0.0 copy-start.2
  2.2 178.6 %shard_map.95 = (f32[192,2048]{1,0:T(8,128)}, f32[192,128]{1,0:T(8,128)}) custom-call(bf16[192,2048]{1,0:T(8,128)(2,1)} %bitcast.37, bf16[192,2048]{1,0:T(8,128)(2,1)} %bitcast.38, s32[8,192]{1,0:T(8,128)} %bitcast.32, f32[8,192]{1,0:T(8,128)} %bitcast.30, bf16[2048,768]{1,0:T(8,128)(2,1)} %bitcast.34, bf16[2048,768]{1,0:T(8,128)(2,1)} %bitcast.35, ...), custom_call_target="tpu_custom_call" | custom-call | flops 12079595520 | bytes 9437184 | tf_op jit(solution)/shard_map/pallas_call | solution.py:472
  180.8 1.4 select_reduce_fusion
  182.2 0.1 copy.21
  182.3 0.0 copy-done.1
  182.3 0.6 fusion.3
  182.9 0.0 copy-done.2
  182.9 0.1 select_reduce_fusion.1
  183.0 0.0 copy-done
  183.0 3.1 %fusion.1 = bf16[1,192,2048]{2,1,0:T(8,128)(2,1)} fusion(f32[192,2048]{1,0:T(8,128)} %get-tuple-element.4, f32[192,64]{0,1:T(8,128)S(1)} %select_reduce_fusion.1, bf16[1,2048,64]{1,2,0:T(8,128)(2,1)S(1)} %copy-done), kind=kOutput, calls=%fused_computation.2 | convolution fusion | flops 302776320 | bytes 2670592 | tf_op jit(solution)/shard_map/dot_general | solution.py:540
  (2 shorter events, 0.0 us)
Async XLA Ops:
  0.6 182.4 %copy-start = (bf16[1,2048,64]{1,2,0:T(8,128)(2,1)S(1)}, bf16[1,2048,64]{1,2,0:T(8,128)(2,1)}, u32[]{:S(2)}) copy-start(bf16[1,2048,64]{1,2,0:T(8,128)(2,1)} %param.15) | copy-start | bytes 786436
  2.2 180.1 %copy-start.1 = (f32[1,192,8]{1,2,0:T(8,128)S(1)}, f32[1,192,8]{1,2,0:T(8,128)}, u32[]{:S(2)}) copy-start(f32[1,192,8]{1,2,0:T(8,128)} %param.11) | copy-start | bytes 18436
  2.2 180.7 %copy-start.2 = (s32[1,192,8]{1,2,0:T(8,128)S(1)}, s32[1,192,8]{1,2,0:T(8,128)}, u32[]{:S(2)}) copy-start(s32[1,192,8]{1,2,0:T(8,128)} %param.10) | copy-start | bytes 18436

commit v5 on v4

--- a/solution.py
+++ b/solution.py
@@ -162,14 +162,17 @@
 
     def do_pack(kind, origin, piece):
         source = both[kind, origin, :, cut(piece)]
-        for step in list(range(1, group)) + [0]:
-            pick = jnp.where(chosen(origin, 0, (q + step) % group) == place, 1.0, 0.0).astype(BF16)
-            packed = jnp.dot(pick, source, preferred_element_type=F32).astype(BF16)
-            if step == 0:
-                rows[kind, origin, q, :, cut(piece)] = packed
-            else:
-                pack[kind, origin, step - 1, :, cut(piece)] = packed
-                pack_copy(kind, origin, step, piece).start()
+        picks = [
+            jnp.where(chosen(origin, 0, (q + step) % group) == place, 1.0, 0.0).astype(BF16)
+            for step in range(group)
+        ]
+        packed = jnp.dot(
+            jnp.concatenate(picks, axis=0), source, preferred_element_type=F32
+        ).astype(BF16)
+        for step in range(1, group):
+            pack[kind, origin, step - 1, :, cut(piece)] = packed[step * cap:(step + 1) * cap]
+            pack_copy(kind, origin, step, piece).start()
+        rows[kind, origin, q, :, cut(piece)] = packed[:cap]
 
     def ret_copy(origin, step, piece):
         slot = (q + group - step) % group
@@ -278,6 +281,9 @@
     keep_x.wait()
     for piece in range(PIECES):
         do_pack(0, p, piece)
+    for copy in weights:
+        copy.wait()
+    do_front(p)
     for step in range(1, LINE):
         meta_wait(step).wait_recv()
 
@@ -294,10 +300,9 @@
     def candidate(n, i):
         valid_up, kind_up, origin_up = arrival(0, i)
         valid_down, kind_down, origin_down = arrival(1, i)
-        own = (i == 0) | (i == -1)
-        valid = jnp.where(n == 0, jnp.where(own, 1, 0), jnp.where(
+        valid = jnp.where(n == 0, jnp.where(i == 0, 1, 0), jnp.where(
             n == 1, jnp.where(valid_up, 1, 0), jnp.where(valid_down, 1, 0)))
-        kind = jnp.where(n == 0, i + 1, jnp.where(n == 1, kind_up, kind_down))
+        kind = jnp.where(n == 0, 1, jnp.where(n == 1, kind_up, kind_down))
         origin = jnp.where(n == 0, p, jnp.where(n == 1, origin_up, origin_down))
         return valid == 1, kind, origin
 
@@ -329,9 +334,11 @@
                     for piece in range(PIECES):
                         line_copy(1, p, way, piece).start()
 
-        def each(step, body):
+        def each(step, body, own_step=None):
             def one(n, carry):
-                valid, kind, origin = candidate(n, step)
+                valid, kind, origin = candidate(
+                    n, step if own_step is None else jnp.where(n == 0, own_step, step)
+                )
                 body(valid, kind, origin)
                 return carry
 
@@ -362,19 +369,14 @@
             if piece == PIECES - 1:
                 own_gradients()
             each(i, functools.partial(pack_one, piece))
-
-        @pl.when(i == 0)
-        def _():
-            for copy in weights:
-                copy.wait()
-
-        each(i - 1, front_one)
-
-        @pl.when(late == 0)
-        def _():
-            each(i - 1, combine_one)
-
-        each(i - late, back_one)
+            if piece == 0:
+                each(i - 1, front_one)
+
+                @pl.when(late == 0)
+                def _():
+                    each(i - 1, combine_one)
+
+        each(i - late, back_one, i)
 
         @pl.when(late == 1)
         def _():

time: 186 us -> 186 us (level)
  Pallas kernels: 179 us -> 177 us
where the time goes in v5:
time: 186 us; the launch traced here: 185 us
  Pallas kernels  177 us (95%)
  matrix products  3.13 us (2%)
  other arithmetic  2.87 us (2%)
    pallas_call x1, Pallas kernels, exchange(): pl.pallas_call(functools.partial(kernel, sections, experts, cap), out_sha...  177 us

profile of v5, /device:TPU:18, one launch (start us, length us, event | category | flops | bytes accessed | tf_op | source)
XLA Modules:
  0.0 185.0 jit_solution(14545132222912027094)
XLA Ops:
  0.6 0.0 copy-start
  0.6 0.8 fusion.5
  1.4 0.8 copy.19
  2.2 0.0 copy-start.1
  2.2 0.0 copy-start.2
  2.2 177.4 %shard_map.95 = (f32[192,2048]{1,0:T(8,128)}, f32[192,128]{1,0:T(8,128)}) custom-call(bf16[192,2048]{1,0:T(8,128)(2,1)} %bitcast.37, bf16[192,2048]{1,0:T(8,128)(2,1)} %bitcast.38, s32[8,192]{1,0:T(8,128)} %bitcast.32, f32[8,192]{1,0:T(8,128)} %bitcast.30, bf16[2048,768]{1,0:T(8,128)(2,1)} %bitcast.34, bf16[2048,768]{1,0:T(8,128)(2,1)} %bitcast.35, ...), custom_call_target="tpu_custom_call" | custom-call | flops 12079595520 | bytes 9437184 | tf_op jit(solution)/shard_map/pallas_call | solution.py:474
  179.7 1.4 select_reduce_fusion
  181.1 0.1 copy.21
  181.1 0.0 copy-done.1
  181.1 0.6 fusion.3
  181.8 0.0 copy-done.2
  181.8 0.1 select_reduce_fusion.1
  181.9 0.0 copy-done
  181.9 3.1 %fusion.1 = bf16[1,192,2048]{2,1,0:T(8,128)(2,1)} fusion(f32[192,2048]{1,0:T(8,128)} %get-tuple-element.4, f32[192,64]{0,1:T(8,128)S(1)} %select_reduce_fusion.1, bf16[1,2048,64]{1,2,0:T(8,128)(2,1)S(1)} %copy-done), kind=kOutput, calls=%fused_computation.2 | convolution fusion | flops 302776320 | bytes 2670592 | tf_op jit(solution)/shard_map/dot_general | solution.py:542
  (2 shorter events, 0.0 us)
Async XLA Ops:
  0.6 181.2 %copy-start = (bf16[1,2048,64]{1,2,0:T(8,128)(2,1)S(1)}, bf16[1,2048,64]{1,2,0:T(8,128)(2,1)}, u32[]{:S(2)}) copy-start(bf16[1,2048,64]{1,2,0:T(8,128)(2,1)} %param.15) | copy-start | bytes 786436
  2.2 178.9 %copy-start.1 = (f32[1,192,8]{1,2,0:T(8,128)S(1)}, f32[1,192,8]{1,2,0:T(8,128)}, u32[]{:S(2)}) copy-start(f32[1,192,8]{1,2,0:T(8,128)} %param.11) | copy-start | bytes 18436
  2.2 179.6 %copy-start.2 = (s32[1,192,8]{1,2,0:T(8,128)S(1)}, s32[1,192,8]{1,2,0:T(8,128)}, u32[]{:S(2)}) copy-start(s32[1,192,8]{1,2,0:T(8,128)} %param.10) | copy-start | bytes 18436

commit v6 on v5

--- a/solution.py
+++ b/solution.py
@@ -334,11 +334,9 @@
                     for piece in range(PIECES):
                         line_copy(1, p, way, piece).start()
 
-        def each(step, body, own_step=None):
+        def each(step, body):
             def one(n, carry):
-                valid, kind, origin = candidate(
-                    n, step if own_step is None else jnp.where(n == 0, own_step, step)
-                )
+                valid, kind, origin = candidate(n, step)
                 body(valid, kind, origin)
                 return carry
 
@@ -376,7 +374,7 @@
                 def _():
                     each(i - 1, combine_one)
 
-        each(i - late, back_one, i)
+        each(i - late, back_one)
 
         @pl.when(late == 1)
         def _():

time: 186 us -> 186 us (level)
  no operation moved by 1% of the time
where the time goes in v6:
time: 186 us; the launch traced here: 185 us
  Pallas kernels  177 us (95%)
  matrix products  3.13 us (2%)
  other arithmetic  2.87 us (2%)
    pallas_call x1, Pallas kernels, exchange(): pl.pallas_call(functools.partial(kernel, sections, experts, cap), out_sha...  177 us

profile of v6, /device:TPU:18, one launch (start us, length us, event | category | flops | bytes accessed | tf_op | source)
XLA Modules:
  0.0 185.0 jit_solution(12835307202596905195)
XLA Ops:
  0.6 0.0 copy-start
  0.6 0.8 fusion.5
  1.4 0.8 copy.19
  2.2 0.0 copy-start.1
  2.2 0.0 copy-start.2
  2.2 177.4 %shard_map.95 = (f32[192,2048]{1,0:T(8,128)}, f32[192,128]{1,0:T(8,128)}) custom-call(bf16[192,2048]{1,0:T(8,128)(2,1)} %bitcast.37, bf16[192,2048]{1,0:T(8,128)(2,1)} %bitcast.38, s32[8,192]{1,0:T(8,128)} %bitcast.32, f32[8,192]{1,0:T(8,128)} %bitcast.30, bf16[2048,768]{1,0:T(8,128)(2,1)} %bitcast.34, bf16[2048,768]{1,0:T(8,128)(2,1)} %bitcast.35, ...), custom_call_target="tpu_custom_call" | custom-call | flops 12079595520 | bytes 9437184 | tf_op jit(solution)/shard_map/pallas_call | solution.py:472
  179.7 1.4 select_reduce_fusion
  181.1 0.1 copy.21
  181.1 0.0 copy-done.1
  181.1 0.6 fusion.3
  181.8 0.0 copy-done.2
  181.8 0.1 select_reduce_fusion.1
  181.9 0.0 copy-done
  181.9 3.1 %fusion.1 = bf16[1,192,2048]{2,1,0:T(8,128)(2,1)} fusion(f32[192,2048]{1,0:T(8,128)} %get-tuple-element.4, f32[192,64]{0,1:T(8,128)S(1)} %select_reduce_fusion.1, bf16[1,2048,64]{1,2,0:T(8,128)(2,1)S(1)} %copy-done), kind=kOutput, calls=%fused_computation.2 | convolution fusion | flops 302776320 | bytes 2670592 | tf_op jit(solution)/shard_map/dot_general | solution.py:540
  (2 shorter events, 0.0 us)
Async XLA Ops:
  0.6 181.2 %copy-start = (bf16[1,2048,64]{1,2,0:T(8,128)(2,1)S(1)}, bf16[1,2048,64]{1,2,0:T(8,128)(2,1)}, u32[]{:S(2)}) copy-start(bf16[1,2048,64]{1,2,0:T(8,128)(2,1)} %param.15) | copy-start | bytes 786436
  2.2 178.9 %copy-start.1 = (f32[1,192,8]{1,2,0:T(8,128)S(1)}, f32[1,192,8]{1,2,0:T(8,128)}, u32[]{:S(2)}) copy-start(f32[1,192,8]{1,2,0:T(8,128)} %param.11) | copy-start | bytes 18436
  2.2 179.6 %copy-start.2 = (s32[1,192,8]{1,2,0:T(8,128)S(1)}, s32[1,192,8]{1,2,0:T(8,128)}, u32[]{:S(2)}) copy-start(s32[1,192,8]{1,2,0:T(8,128)} %param.10) | copy-start | bytes 18436
